TPU v7x, 256 devices: a whole 4x4x8 slice. The times are simulated.
256 devices in a mesh: seq: 64 (over z_hi, y, x), ch: 4 (over z_lo, core).
Axes of the slice: x: 4, y: 4, z: 8 (z_hi: 4, z_lo: 2; z = z_hi * 2 + z_lo), core: 2. Of those that a mesh axis runs over, the one named last changes fastest.
Arguments:
- output_gate: bfloat16 [8192, 4096], P('seq', 'ch'), may hold values from -6 to 6
- input_gate: bfloat16 [8192, 4096], P('seq', 'ch'), may hold values from -6 to 6
- values_in: bfloat16 [8192, 4096], P('seq', 'ch'), may hold values from -6 to 6
- filters: bfloat16 [8192, 4096], P(None, ('seq', 'ch')), may hold values from -6 to 6
- cotangent: bfloat16 [8192, 4096], P('seq', 'ch'), may hold values from -6 to 6
Outputs:
- output: bfloat16 [8192, 4096], P('seq', 'ch')
- grad_output_gate: bfloat16 [8192, 4096], P('seq', 'ch')
- grad_input_gate: bfloat16 [8192, 4096], P('seq', 'ch')
- grad_values: bfloat16 [8192, 4096], P('seq', 'ch')
- grad_filters: float32 [8192, 4096], P(None, ('seq', 'ch'))
All inputs are finite; a program needn't handle non-finite values.
Results may differ from a plain program's by a relative error of at most 0.0058.
Values may be sent and summed in bfloat16 or wider, within the bound.
No kernel may reach another device: no remote copies, remote signals or barrier semaphores. Data moves between devices by JAX's collectives and lax.ppermute only.
A program may use at most 64 MiB of HBM per device.

v0:
```python
import math

import jax
import jax.numpy as jnp
from jax import lax
from jax.experimental import pallas as pl
from jax.experimental.pallas import tpu as pltpu
from jax.sharding import PartitionSpec as P

LANES = 128
ROWS = 16
WIDE = jnp.float32
NARROW = jnp.bfloat16


def exchange_matrix():
    row = lax.broadcasted_iota(jnp.int32, (LANES, LANES), 0)
    col = lax.broadcasted_iota(jnp.int32, (LANES, LANES), 1)
    return (row + col == LANES - 1).astype(NARROW)


def gate_kernel(out_gate, in_gate, values, cotan, send):
    groups, per_group, _, owned, _ = send.shape
    mixed = (in_gate[...].astype(WIDE) * values[...].astype(WIDE)).astype(NARROW)
    gated = (cotan[...].astype(WIDE) * out_gate[...].astype(WIDE)).astype(NARROW)
    flipped = jnp.dot(exchange_matrix(), gated, preferred_element_type=WIDE)
    for which, array in enumerate((mixed.astype(WIDE), flipped)):
        turned = array.T.astype(NARROW).reshape(per_group, groups, owned, LANES)
        for g in range(groups):
            send[g, :, which] = turned[:, g]


def gates(out_gate, in_gate, values, cotan, seq_count, chan_count):
    width = out_gate.shape[1]
    groups = chan_count
    per_group = seq_count // chan_count
    owned = width // seq_count
    steps = 4
    block = pl.BlockSpec((LANES, width // steps), lambda i: (0, i))
    return pl.pallas_call(
        gate_kernel,
        grid=(steps,),
        in_specs=[block] * 4,
        out_specs=pl.BlockSpec((groups, per_group // steps, 2, owned, LANES), lambda i: (0, i, 0, 0, 0)),
        out_shape=jax.ShapeDtypeStruct((groups, per_group, 2, owned, LANES), NARROW),
        name="gate_products",
    )(out_gate, in_gate, values, cotan)


def toeplitz(load_block, matrix, blocks):
    lane = lax.broadcasted_iota(jnp.int32, (ROWS, LANES), 1)
    row = lax.broadcasted_iota(jnp.int32, (ROWS, LANES), 0)
    tiles = LANES // ROWS
    zero = jnp.zeros((ROWS, LANES), NARROW)
    turned_before = jnp.zeros((ROWS, LANES), WIDE)
    before = [zero] * tiles
    for q in range(blocks):
        source = jnp.broadcast_to(load_block(q), (ROWS, LANES))
        turned = pltpu.roll(source, 0, axis=1, stride=1, stride_axis=0)
        base = jnp.where(lane >= row, turned, turned_before).astype(NARROW)
        turned_before = turned
        now = []
        for k in range(tiles):
            piece = base if k == 0 else pltpu.roll(base, ROWS * k, axis=1)
            tile = base if k == 0 else jnp.where(lane >= ROWS * k, piece, before[k])
            matrix[pl.ds(LANES * q + ROWS * k, ROWS), :] = tile
            now.append(piece)
        before = now


def causal_product(shifted, matrix, blocks):
    height = blocks // ROWS
    rows = shifted.shape[1]
    depth = ROWS * LANES
    parts = []
    for step in range(height):
        left = shifted[0 : height - step].reshape((height - step) * rows, depth)
        product = jnp.dot(
            left, matrix[pl.ds(step * depth, depth), :], preferred_element_type=WIDE
        ).reshape(height - step, rows, LANES)
        for at in range(height - step):
            if step == 0:
                parts.append(product[at])
            else:
                parts[at + step] = parts[at + step] + product[at]
    return parts


def conv_kernel(
    scale, received, filters, send, grad_filters, signal, taps, back, grads, shifted, matrix
):
    blocks, _, owned, _ = received.shape
    height = blocks // ROWS
    pad = ROWS * owned
    for which in range(2):
        signal[which, pl.ds(0, pad), :] = jnp.zeros((pad, LANES), WIDE)
    for j in range(blocks):
        signal[0, pl.ds(pad + j * owned, owned), :] = received[j, 0].astype(WIDE)
        signal[1, pl.ds(pad + j * owned, owned), :] = received[blocks - 1 - j, 1].astype(WIDE)
    for q in range(blocks):
        taps[pl.ds(q * owned, owned), :] = filters[:, pl.ds(q * LANES, LANES)].astype(WIDE)

    def channel(c, carry):
        for which in range(2):
            for r in range(ROWS):
                rows = signal[which, pl.ds(c + (ROWS - r) * owned, blocks, stride=owned), :]
                rows = rows.astype(NARROW).reshape(height, ROWS, LANES)
                shifted[:, which, :, pl.ds(r * LANES, LANES)] = rows
        toeplitz(lambda q: taps[pl.ds(q * owned + c, 1), :], matrix, blocks)
        both = causal_product(
            shifted[...].reshape(height, 2 * ROWS, ROWS * LANES), matrix, blocks
        )
        for at in range(height):
            forth = (at * ROWS) * owned + c
            back[0, pl.ds(forth, ROWS, stride=owned), :] = both[at][:ROWS] * scale
            back[1, pl.ds(forth, ROWS, stride=owned), :] = both[at][ROWS:] * scale
        toeplitz(
            lambda q: signal[0, pl.ds(pad + q * owned + c, 1), :], matrix, blocks
        )
        grad = causal_product(shifted[:, 1], matrix, blocks)
        for at in range(height):
            grads[pl.ds((at * ROWS) * owned + c, ROWS, stride=owned), :] = grad[at] * scale
        return carry

    lax.fori_loop(0, owned, channel, 0)
    conv = back[0].reshape(blocks, owned, LANES).astype(NARROW)
    grad_mixed = back[1].reshape(blocks, owned, LANES).astype(NARROW)
    for j in range(blocks):
        send[j, 0] = conv[j]
        send[j, 1] = grad_mixed[blocks - 1 - j]
    grad_filters[...] = grads[...].reshape(blocks, owned, LANES).astype(NARROW)


def convolutions(received, filters, scale):
    blocks, _, owned, _ = received.shape
    length = blocks * LANES
    vmem = pl.BlockSpec(memory_space=pltpu.VMEM)
    return pl.pallas_call(
        lambda *refs: conv_kernel(scale, *refs),
        in_specs=[vmem, vmem],
        out_specs=[vmem, vmem],
        out_shape=[
            jax.ShapeDtypeStruct(received.shape, NARROW),
            jax.ShapeDtypeStruct((blocks, owned, LANES), NARROW),
        ],
        scratch_shapes=[
            pltpu.VMEM((2, (ROWS + blocks) * owned, LANES), WIDE),
            pltpu.VMEM((blocks * owned, LANES), WIDE),
            pltpu.VMEM((2, blocks * owned, LANES), WIDE),
            pltpu.VMEM((blocks * owned, LANES), WIDE),
            pltpu.VMEM((blocks // ROWS, 2, ROWS, ROWS * LANES), NARROW),
            pltpu.VMEM((length, LANES), NARROW),
        ],
        compiler_params=pltpu.CompilerParams(vmem_limit_bytes=32 * 1024 * 1024),
        name="convolutions",
    )(received, filters)


def result_kernel(out_gate, in_gate, values, cotan, received, output, grad_out, grad_in, grad_values):
    groups, per_group, _, owned, _ = received.shape
    turned = []
    for which in range(2):
        pieces = [received[g, :, which] for g in range(groups)]
        array = jnp.stack(pieces, axis=1).reshape(groups * per_group * owned, LANES)
        turned.append(array.astype(WIDE).T)
    conv = turned[0]
    grad_mixed = jnp.dot(
        exchange_matrix(), turned[1].astype(NARROW), preferred_element_type=WIDE
    )
    output[...] = (out_gate[...].astype(WIDE) * conv).astype(NARROW)
    grad_out[...] = (cotan[...].astype(WIDE) * conv).astype(NARROW)
    grad_in[...] = (grad_mixed * values[...].astype(WIDE)).astype(NARROW)
    grad_values[...] = (grad_mixed * in_gate[...].astype(WIDE)).astype(NARROW)


def results(out_gate, in_gate, values, cotan, received):
    groups, per_group, _, owned, _ = received.shape
    width = out_gate.shape[1]
    steps = 4
    block = pl.BlockSpec((LANES, width // steps), lambda i: (0, i))
    return pl.pallas_call(
        result_kernel,
        grid=(steps,),
        in_specs=[block] * 4
        + [pl.BlockSpec((groups, per_group // steps, 2, owned, LANES), lambda i: (0, i, 0, 0, 0))],
        out_specs=[block] * 4,
        out_shape=[jax.ShapeDtypeStruct(out_gate.shape, NARROW)] * 4,
        name="gate_results",
    )(out_gate, in_gate, values, cotan, received)


def filter_kernel(received, grad_filters):
    blocks, owned, _ = received.shape
    flat = received[...].reshape(blocks * owned, LANES)
    flipped = jnp.dot(flat, exchange_matrix(), preferred_element_type=WIDE)
    flipped = flipped.reshape(blocks, owned, LANES)
    for j in range(blocks):
        grad_filters[:, pl.ds(j * LANES, LANES)] = flipped[blocks - 1 - j]


def filter_results(received):
    blocks, owned, _ = received.shape
    return pl.pallas_call(
        filter_kernel,
        out_shape=jax.ShapeDtypeStruct((owned, blocks * LANES), WIDE),
        name="filter_results",
    )(received)


def per_device(output_gate, input_gate, values_in, filters, cotangent):
    seq_count = lax.axis_size("seq")
    chan_count = lax.axis_size("ch")
    per_group = seq_count // chan_count
    length, owned = filters.shape
    scale = 1.0 / math.sqrt(length)
    swap = []
    for s in range(seq_count):
        for c in range(chan_count):
            high, low = divmod(s, per_group)
            swap.append((s * chan_count + c, (c * per_group + low) * chan_count + high))
    filters_here = lax.ppermute(filters.T, ("seq", "ch"), swap)
    send = gates(output_gate, input_gate, values_in, cotangent, seq_count, chan_count)
    sections = send.reshape(seq_count, 2, owned, LANES)
    received = lax.all_to_all(sections, "seq", split_axis=0, concat_axis=0, tiled=True)
    back, grads = convolutions(received, filters_here, scale)
    grads_owned = lax.ppermute(grads, ("seq", "ch"), swap)
    returned = lax.all_to_all(back, "seq", split_axis=0, concat_axis=0, tiled=True)
    returned = returned.reshape(chan_count, per_group, 2, owned, LANES)
    grad_filters = filter_results(grads_owned).T
    output, grad_out, grad_in, grad_values = results(
        output_gate, input_gate, values_in, cotangent, returned
    )
    return (output, grad_out, grad_in, grad_values, grad_filters)


def solution(mesh):
    by_position = P("seq", "ch")
    by_channel = P(None, ("seq", "ch"))
    return jax.shard_map(
        per_device,
        mesh=mesh,
        in_specs=(by_position, by_position, by_position, by_channel, by_position),
        out_specs=(by_position, by_position, by_position, by_position, by_channel),
        check_vma=False,
    )
```

profile of v0, /device:TPU:32, one launch (start us, length us, event | category | flops | bytes accessed | tf_op | source)
XLA Modules:
  0.0 158.4 jit_solution(2287887720990021270)
XLA Ops:
  0.6 3.7 %gate_products.1 = bf16[4,16,2,16,128]{4,3,2,1,0:T(8,128)(2,1)} custom-call(bf16[128,1024]{1,0:T(8,128)(2,1)} %out_gate.3, bf16[128,1024]{1,0:T(8,128)(2,1)} %in_gate.3, bf16[128,1024]{1,0:T(8,128)(2,1)} %values.3, bf16[128,1024]{1,0:T(8,128)(2,1)} %cotan.3), custom_call_target="tpu_custom_call" | custom-call | tf_op jit(solution)/shard_map/gate_products/pallas_call | solution.py:40
  4.4 0.0 copy-start.2
  4.4 13.8 %all-to-all-start = ((bf16[64,2,16,128]{3,2,1,0:T(8,128)(2,1)}), bf16[64,2,16,128]{3,2,1,0:T(8,128)(2,1)S(1)}, u32[]{:S(2)}, u32[]{:S(2)}) async-start(bf16[64,2,16,128]{3,2,1,0:T(8,128)(2,1)} %bitcast.5), calls=%async_computation | async-start | bytes 1048576 | tf_op jit(solution)/shard_map/all_to_all | solution.py:224
  18.2 0.0 copy-done.2
  18.2 7.0 %collective-permute-start = (bf16[16,8192]{1,0:T(8,128)(2,1)S(1)}, bf16[16,8192]{1,0:T(8,128)(2,1)S(1)}, u32[]{:S(2)}, u32[]{:S(2)}) collective-permute-start(bf16[16,8192]{1,0:T(8,128)(2,1)S(1)} %bitcast.7), channel_id=1, source_target_pairs={{0,0},{1,64},{2,128},{3,192},{4,4},{5,68},{6,132},{7,196},{8,8},{9... | collective-permute-start | bytes 786440 | tf_op jit(solution)/shard_map/ppermute | solution.py:221
  25.2 17.7 %collective-permute-done.refs_1_ = bf16[16,8192]{1,0:T(8,128)(2,1)S(1)} collective-permute-done((bf16[16,8192]{1,0:T(8,128)(2,1)S(1)}, bf16[16,8192]{1,0:T(8,128)(2,1)S(1)}, u32[]{:S(2)}, u32[]{:S(2)}) %collective-permute-start) | collective-permute-done | bytes 262176 | tf_op jit(solution)/shard_map/ppermute | solution.py:221
  42.9 0.0 all-to-all-done.refs_0_
  42.9 77.9 %convolutions.1 = (bf16[64,2,16,128]{3,2,1,0:T(8,128)(2,1)}, bf16[64,16,128]{2,1,0:T(8,128)(2,1)S(1)}) custom-call(bf16[64,2,16,128]{3,2,1,0:T(8,128)(2,1)S(1)} %all-to-all-done.refs_0_, bf16[16,8192]{1,0:T(8,128)(2,1)S(1)} %collective-permute-done.refs_1_), custom_call_target="tpu_custom_call" | custom-call | tf_op jit(solution)/shard_map/convolutions/pallas_call | solution.py:138
  120.8 7.7 %all-to-all-start.1 = ((bf16[64,2,16,128]{3,2,1,0:T(8,128)(2,1)}), bf16[64,2,16,128]{3,2,1,0:T(8,128)(2,1)S(1)}, u32[]{:S(2)}, u32[]{:S(2)}) async-start(bf16[64,2,16,128]{3,2,1,0:T(8,128)(2,1)} %get-tuple-element.11), calls=%async_computation.1 | async-start | bytes 1048576 | tf_op jit(solution)/shard_map/all_to_all | solution.py:227
  128.6 6.5 %collective-permute-start.1 = (bf16[64,16,128]{2,1,0:T(8,128)(2,1)S(1)}, bf16[64,16,128]{2,1,0:T(8,128)(2,1)S(1)}, u32[]{:S(2)}, u32[]{:S(2)}) collective-permute-start(bf16[64,16,128]{2,1,0:T(8,128)(2,1)S(1)} %get-tuple-element.16), channel_id=1, source_target_pairs={{0,0},{1,64},{2,128},{3,192},{4,4},{5,68},{6,132},{7,196},{8,8},{9... | collective-permute-start | bytes 786440 | tf_op jit(solution)/shard_map/ppermute | solution.py:226
  135.0 16.0 %collective-permute-done.1.received = bf16[64,16,128]{2,1,0:T(8,128)(2,1)S(1)} collective-permute-done((bf16[64,16,128]{2,1,0:T(8,128)(2,1)S(1)}, bf16[64,16,128]{2,1,0:T(8,128)(2,1)S(1)}, u32[]{:S(2)}, u32[]{:S(2)}) %collective-permute-start.1) | collective-permute-done | bytes 262176 | tf_op jit(solution)/shard_map/ppermute | solution.py:226
  151.1 0.0 copy-start.1
  151.1 0.7 copy-done.1
  151.8 2.0 %filter_results.1 = f32[16,8192]{1,0:T(8,128)} custom-call(bf16[64,16,128]{2,1,0:T(8,128)(2,1)} %copy-done.1), custom_call_target="tpu_custom_call" | custom-call | tf_op jit(solution)/shard_map/filter_results/pallas_call | solution.py:203
  153.7 0.0 all-to-all-done.1
  153.7 0.0 copy-start
  153.7 0.8 copy-done
  154.5 3.9 %gate_results.1 = (bf16[128,1024]{1,0:T(8,128)(2,1)}, bf16[128,1024]{1,0:T(8,128)(2,1)}, bf16[128,1024]{1,0:T(8,128)(2,1)}, bf16[128,1024]{1,0:T(8,128)(2,1)}) custom-call(bf16[128,1024]{1,0:T(8,128)(2,1)} %out_gate.3, bf16[128,1024]{1,0:T(8,128)(2,1)} %in_gate.3, bf16[128,1024]{1,0:T(8,128)(2,1)} %values.3, bf16[128,1024]{1,0:T(8,128)(2,1)} %cotan.3, ...), custom_call_target="tpu_custom_call" | custom-call | tf_op jit(solution)/shard_map/gate_results/pallas_call | solution.py:181
Async XLA Ops:
  4.4 13.8 %copy-start.2 = (bf16[8192,16]{0,1:T(8,128)(2,1)S(1)}, bf16[8192,16]{0,1:T(8,128)(2,1)}, u32[]{:S(2)}) copy-start(bf16[8192,16]{0,1:T(8,128)(2,1)} %param.8) | copy-start | bytes 786436
  4.4 38.6 %all-to-all-start = ((bf16[64,2,16,128]{3,2,1,0:T(8,128)(2,1)}), bf16[64,2,16,128]{3,2,1,0:T(8,128)(2,1)S(1)}, u32[]{:S(2)}, u32[]{:S(2)}) async-start(bf16[64,2,16,128]{3,2,1,0:T(8,128)(2,1)} %bitcast.5), calls=%async_computation | async-start | bytes 1048576 | tf_op jit(solution)/shard_map/all_to_all | solution.py:224
  18.2 24.7 %collective-permute-start = (bf16[16,8192]{1,0:T(8,128)(2,1)S(1)}, bf16[16,8192]{1,0:T(8,128)(2,1)S(1)}, u32[]{:S(2)}, u32[]{:S(2)}) collective-permute-start(bf16[16,8192]{1,0:T(8,128)(2,1)S(1)} %bitcast.7), channel_id=1, source_target_pairs={{0,0},{1,64},{2,128},{3,192},{4,4},{5,68},{6,132},{7,196},{8,8},{9... | collective-permute-start | bytes 786440 | tf_op jit(solution)/shard_map/ppermute | solution.py:221
  120.8 32.9 %all-to-all-start.1 = ((bf16[64,2,16,128]{3,2,1,0:T(8,128)(2,1)}), bf16[64,2,16,128]{3,2,1,0:T(8,128)(2,1)S(1)}, u32[]{:S(2)}, u32[]{:S(2)}) async-start(bf16[64,2,16,128]{3,2,1,0:T(8,128)(2,1)} %get-tuple-element.11), calls=%async_computation.1 | async-start | bytes 1048576 | tf_op jit(solution)/shard_map/all_to_all | solution.py:227
  128.6 22.5 %collective-permute-start.1 = (bf16[64,16,128]{2,1,0:T(8,128)(2,1)S(1)}, bf16[64,16,128]{2,1,0:T(8,128)(2,1)S(1)}, u32[]{:S(2)}, u32[]{:S(2)}) collective-permute-start(bf16[64,16,128]{2,1,0:T(8,128)(2,1)S(1)} %get-tuple-element.16), channel_id=1, source_target_pairs={{0,0},{1,64},{2,128},{3,192},{4,4},{5,68},{6,132},{7,196},{8,8},{9... | collective-permute-start | bytes 786440 | tf_op jit(solution)/shard_map/ppermute | solution.py:226
  151.1 0.7 copy-start.1
  153.7 0.8 copy-start
where the time goes:
time: 159 us; the launch traced here: 158 us
  Pallas kernels  87.5 us (55%)
  starting transfers between devices  35 us (22%)
  waiting for transfers between devices  33.7 us (21%)
    pallas_call x1, Pallas kernels, convolutions(): pl.pallas_call(lambda *refs: conv_kernel(scale, *refs), in_specs=[vmem, v...  77.9 us
    ppermute x1, waiting for transfers between devices, per_device(): filters_here = lax.ppermute(filters.T, ('seq', 'ch'), swap)  17.7 us
    ppermute x1, waiting for transfers between devices, per_device(): grads_owned = lax.ppermute(grads, ('seq', 'ch'), swap)  16 us
    all_to_all x1, starting transfers between devices, per_device(): lax.all_to_all(sections, 'seq', split_axis=0, concat_axis=0, tiled=True)  13.8 us
    all_to_all x1, starting transfers between devices, per_device(): lax.all_to_all(back, 'seq', split_axis=0, concat_axis=0, tiled=True)  7.73 us
    ppermute x1, starting transfers between devices, per_device(): filters_here = lax.ppermute(filters.T, ('seq', 'ch'), swap)  7.03 us
    ppermute x1, starting transfers between devices, per_device(): grads_owned = lax.ppermute(grads, ('seq', 'ch'), swap)  6.47 us
    pallas_call x1, Pallas kernels, results(): pl.pallas_call(result_kernel, grid=(steps,), in_specs=[block] * 4 + [pl.B...  3.91 us
  transfers between devices with their start and end apart: 4, of which 2 were waited for; matrix products, arithmetic and copies ran while one was open for 0% of the time, Pallas kernels for 1%

commit v1 on v0

v1 whole, which is shorter than its diff:
```python
import functools
import math

import jax
import jax.numpy as jnp
import numpy as np
from jax import lax
from jax.experimental import pallas as pl
from jax.experimental.pallas import tpu as pltpu
from jax.sharding import PartitionSpec as P

LANES = 128
TOGETHER = 2
WIDE = jnp.float32
NARROW = jnp.bfloat16


def exchange_matrix():
    row = lax.broadcasted_iota(jnp.int32, (LANES, LANES), 0)
    col = lax.broadcasted_iota(jnp.int32, (LANES, LANES), 1)
    return (row + col == LANES - 1).astype(NARROW)


def gate_kernel(out_gate, in_gate, values, cotan, send):
    groups, per_group, _, owned, _ = send.shape
    mixed = (in_gate[...].astype(WIDE) * values[...].astype(WIDE)).astype(NARROW)
    gated = (cotan[...].astype(WIDE) * out_gate[...].astype(WIDE)).astype(NARROW)
    flipped = jnp.dot(exchange_matrix(), gated, preferred_element_type=WIDE)
    for which, array in enumerate((mixed.astype(WIDE), flipped)):
        turned = array.T.astype(NARROW).reshape(per_group, groups, owned, LANES)
        for g in range(groups):
            send[g, :, which] = turned[:, g]


def gates(out_gate, in_gate, values, cotan, seq_count, chan_count):
    width = out_gate.shape[1]
    groups = chan_count
    per_group = seq_count // chan_count
    owned = width // seq_count
    steps = 4
    block = pl.BlockSpec((LANES, width // steps), lambda i: (0, i))
    return pl.pallas_call(
        gate_kernel,
        grid=(steps,),
        in_specs=[block] * 4,
        out_specs=pl.BlockSpec((groups, per_group // steps, 2, owned, LANES), lambda i: (0, i, 0, 0, 0)),
        out_shape=jax.ShapeDtypeStruct((groups, per_group, 2, owned, LANES), NARROW),
        name="gate_products",
    )(out_gate, in_gate, values, cotan)


def split(array):
    high = array.astype(NARROW)
    low = (array - high.astype(WIDE)).astype(NARROW)
    return high, low


def split_table(array):
    high = array.astype(NARROW)
    low = (array - high.astype(np.float64)).astype(NARROW)
    return high, low


def dft_tables(blocks):
    padded = LANES * LANES
    index = np.arange(LANES)
    angle = 2.0 * np.pi / LANES * (index[:, None] * index[None, :] % LANES)
    cos, sin = np.cos(angle), np.sin(angle)
    near_cos, near_sin = cos[:, :blocks], sin[:, :blocks]
    turn = 2.0 * np.pi / padded * (index[:, None] * index[None, :])

    def across(table, order):
        parts = split_table(table)
        return np.concatenate([parts[at] for at in order], axis=1)

    def down(table, order):
        parts = split_table(table)
        return np.concatenate([parts[at] for at in order], axis=0)

    return {
        "first": across(np.block([[near_cos, near_sin], [-near_sin, near_cos]]), (0, 1)),
        "first_real": across(np.block([[near_cos], [-near_sin]]), (0, 1)),
        "second": down(np.block([[cos, -sin], [sin, cos]]), (0, 0, 1)),
        "second_back": down(np.block([[cos, sin], [-sin, cos]]), (0, 0, 1)),
        "first_back": across(
            np.block([[near_cos.T, -near_sin.T], [near_sin.T, near_cos.T]]), (0, 0, 1)
        ),
        "first_back_imag": across(np.block([[near_sin.T, near_cos.T]]), (0, 0, 1)),
        "turn_cos": np.cos(turn).astype(np.float32),
        "turn_sin": np.sin(turn).astype(np.float32),
    }


def dot(left, right):
    return jnp.dot(left, right, preferred_element_type=WIDE)


def three_parts(real, imag, axis):
    real_high, real_low = split(real)
    imag_high, imag_low = split(imag)
    return jnp.concatenate(
        [real_high, imag_high, real_low, imag_low, real_high, imag_high], axis=axis
    )


def spectra(data, first, second, turn_cos, turn_sin):
    stacked = jnp.concatenate([jnp.concatenate([one, one], axis=0) for one in data], axis=1)
    sections = dot(first[...], stacked)
    out = []
    for at in range(len(data)):
        real = sections[:LANES, at * LANES : (at + 1) * LANES]
        imag = sections[LANES:, at * LANES : (at + 1) * LANES]
        turned_real = real * turn_cos[...] + imag * turn_sin[...]
        turned_imag = imag * turn_cos[...] - real * turn_sin[...]
        spectrum = dot(three_parts(turned_real, turned_imag, 1), second[...])
        out.append(spectrum)
    return out


def signals(spectrum, first_back, second_back, turn_cos, turn_sin):
    turned = []
    for real, imag in spectrum:
        part = dot(three_parts(real, imag, 1), second_back[...])
        real, imag = part[:, :LANES], part[:, LANES:]
        turned_real = real * turn_cos[...] - imag * turn_sin[...]
        turned_imag = imag * turn_cos[...] + real * turn_sin[...]
        turned.append(three_parts(turned_real, turned_imag, 0))
    result = dot(first_back[...], jnp.concatenate(turned, axis=1))
    return [result[:, at * LANES : (at + 1) * LANES] for at in range(len(spectrum))]


def spectrum_kernel(filters, first, second, turn_cos, turn_sin, spectrum, taps):
    owned = filters.shape[0]
    blocks = filters.shape[1] // LANES
    for q in range(blocks):
        taps[pl.ds(q * owned, owned), :] = filters[:, pl.ds(q * LANES, LANES)].astype(WIDE)

    def pair(at, carry):
        data = [
            taps[pl.ds(TOGETHER * at + c, blocks, stride=owned), :].astype(NARROW)
            for c in range(TOGETHER)
        ]
        found = spectra(data, first, second, turn_cos, turn_sin)
        for c in range(TOGETHER):
            spectrum[TOGETHER * at + c] = found[c]
        return carry

    lax.fori_loop(0, owned // TOGETHER, pair, 0)


def power_of_two(size):
    exponent = jnp.floor(jnp.log2(jnp.maximum(size, 1e-30)))
    down = jnp.exp2(-exponent).astype(NARROW).astype(WIDE)
    up = jnp.exp2(exponent).astype(NARROW).astype(WIDE)
    return down, up


def convolution_kernel(
    scale,
    received,
    filter_spectrum,
    first,
    second,
    first_back,
    second_back,
    turn_cos,
    turn_sin,
    send,
    own_spectrum,
    sizes,
    signal,
    back,
):
    blocks, _, owned, _ = received.shape
    for which in range(2):
        size = jnp.zeros((owned, LANES), WIDE)
        for j in range(blocks):
            size = jnp.maximum(size, jnp.abs(received[j, which].astype(WIDE)))
        size = jnp.broadcast_to(jnp.max(size, axis=1, keepdims=True), (owned, LANES))
        down, up = power_of_two(size)
        sizes[which] = up
        for j in range(blocks):
            at = j if which == 0 else blocks - 1 - j
            signal[which, pl.ds(at * owned, owned), :] = received[j, which].astype(WIDE) * down

    def pair(at, carry):
        data = []
        for c in range(TOGETHER):
            rows = [
                signal[which, pl.ds(TOGETHER * at + c, blocks, stride=owned), :].astype(NARROW)
                for which in range(2)
            ]
            data.append(jnp.concatenate(rows, axis=0))
        found = spectra(data, first, second, turn_cos, turn_sin)
        products = []
        for c in range(TOGETHER):
            own_spectrum[TOGETHER * at + c] = found[c]
            real, imag = found[c][:, :LANES], found[c][:, LANES:]
            taps_real = filter_spectrum[TOGETHER * at + c, :, :LANES]
            taps_imag = filter_spectrum[TOGETHER * at + c, :, LANES:]
            products.append(
                (real * taps_real - imag * taps_imag, real * taps_imag + imag * taps_real)
            )
        result = signals(products, first_back, second_back, turn_cos, turn_sin)
        for c in range(TOGETHER):
            for which in range(2):
                back[which, pl.ds(TOGETHER * at + c, blocks, stride=owned), :] = result[c][
                    which * blocks : (which + 1) * blocks
                ]
        return carry

    lax.fori_loop(0, owned // TOGETHER, pair, 0)
    for which in range(2):
        up = sizes[which] * scale
        for j in range(blocks):
            at = j if which == 0 else blocks - 1 - j
            send[at, which] = (back[which, pl.ds(j * owned, owned), :] * up).astype(NARROW)


def gradient_kernel(
    scale,
    own_spectrum,
    sizes,
    first_back_imag,
    second_back,
    turn_cos,
    turn_sin,
    grad_filters,
    grads,
):
    blocks, owned, _ = grad_filters.shape

    def pair(at, carry):
        squares = []
        for c in range(TOGETHER):
            real = own_spectrum[TOGETHER * at + c, :, :LANES]
            imag = own_spectrum[TOGETHER * at + c, :, LANES:]
            squares.append((0.5 * (real - imag) * (real + imag), real * imag))
        result = signals(squares, first_back_imag, second_back, turn_cos, turn_sin)
        for c in range(TOGETHER):
            grads[pl.ds(TOGETHER * at + c, blocks, stride=owned), :] = result[c]
        return carry

    lax.fori_loop(0, owned // TOGETHER, pair, 0)
    up = sizes[0] * sizes[1] * scale
    for j in range(blocks):
        grad_filters[j] = (grads[pl.ds(j * owned, owned), :] * up).astype(NARROW)


def in_vmem(count):
    return [pl.BlockSpec(memory_space=pltpu.VMEM)] * count


def params():
    return pltpu.CompilerParams(vmem_limit_bytes=32 * 1024 * 1024)


def filter_spectra(filters, tables):
    owned, length = filters.shape
    return pl.pallas_call(
        spectrum_kernel,
        in_specs=in_vmem(5),
        out_specs=in_vmem(1)[0],
        out_shape=jax.ShapeDtypeStruct((owned, LANES, 2 * LANES), WIDE),
        scratch_shapes=[pltpu.VMEM((length // LANES * owned, LANES), WIDE)],
        compiler_params=params(),
        name="filter_spectra",
    )(filters, tables["first_real"], tables["second"], tables["turn_cos"], tables["turn_sin"])


def convolutions(received, filter_spectrum, tables, scale):
    blocks, _, owned, _ = received.shape
    return pl.pallas_call(
        functools.partial(convolution_kernel, scale / (LANES * LANES)),
        in_specs=in_vmem(8),
        out_specs=in_vmem(3),
        out_shape=[
            jax.ShapeDtypeStruct(received.shape, NARROW),
            jax.ShapeDtypeStruct((owned, LANES, 2 * LANES), WIDE),
            jax.ShapeDtypeStruct((2, owned, LANES), WIDE),
        ],
        scratch_shapes=[
            pltpu.VMEM((2, blocks * owned, LANES), WIDE),
            pltpu.VMEM((2, blocks * owned, LANES), WIDE),
        ],
        compiler_params=params(),
        name="convolutions",
    )(
        received,
        filter_spectrum,
        tables["first"],
        tables["second"],
        tables["first_back"],
        tables["second_back"],
        tables["turn_cos"],
        tables["turn_sin"],
    )


def filter_gradients(own_spectrum, sizes, blocks, tables, scale):
    owned = own_spectrum.shape[0]
    return pl.pallas_call(
        functools.partial(gradient_kernel, scale / (LANES * LANES)),
        in_specs=in_vmem(6),
        out_specs=in_vmem(1)[0],
        out_shape=jax.ShapeDtypeStruct((blocks, owned, LANES), NARROW),
        scratch_shapes=[pltpu.VMEM((blocks * owned, LANES), WIDE)],
        compiler_params=params(),
        name="filter_gradients",
    )(
        own_spectrum,
        sizes,
        tables["first_back_imag"],
        tables["second_back"],
        tables["turn_cos"],
        tables["turn_sin"],
    )


def result_kernel(out_gate, in_gate, values, cotan, received, output, grad_out, grad_in, grad_values):
    groups, per_group, _, owned, _ = received.shape
    turned = []
    for which in range(2):
        pieces = [received[g, :, which] for g in range(groups)]
        array = jnp.stack(pieces, axis=1).reshape(groups * per_group * owned, LANES)
        turned.append(array.astype(WIDE).T)
    conv = turned[0]
    grad_mixed = jnp.dot(
        exchange_matrix(), turned[1].astype(NARROW), preferred_element_type=WIDE
    )
    output[...] = (out_gate[...].astype(WIDE) * conv).astype(NARROW)
    grad_out[...] = (cotan[...].astype(WIDE) * conv).astype(NARROW)
    grad_in[...] = (grad_mixed * values[...].astype(WIDE)).astype(NARROW)
    grad_values[...] = (grad_mixed * in_gate[...].astype(WIDE)).astype(NARROW)


def results(out_gate, in_gate, values, cotan, received):
    groups, per_group, _, owned, _ = received.shape
    width = out_gate.shape[1]
    steps = 4
    block = pl.BlockSpec((LANES, width // steps), lambda i: (0, i))
    return pl.pallas_call(
        result_kernel,
        grid=(steps,),
        in_specs=[block] * 4
        + [pl.BlockSpec((groups, per_group // steps, 2, owned, LANES), lambda i: (0, i, 0, 0, 0))],
        out_specs=[block] * 4,
        out_shape=[jax.ShapeDtypeStruct(out_gate.shape, NARROW)] * 4,
        name="gate_results",
    )(out_gate, in_gate, values, cotan, received)


def filter_kernel(received, grad_filters):
    blocks, owned, _ = received.shape
    flat = received[...].reshape(blocks * owned, LANES)
    flipped = jnp.dot(flat, exchange_matrix(), preferred_element_type=WIDE)
    flipped = flipped.reshape(blocks, owned, LANES)
    for j in range(blocks):
        grad_filters[:, pl.ds(j * LANES, LANES)] = flipped[blocks - 1 - j]


def filter_results(received):
    blocks, owned, _ = received.shape
    return pl.pallas_call(
        filter_kernel,
        out_shape=jax.ShapeDtypeStruct((owned, blocks * LANES), WIDE),
        name="filter_results",
    )(received)


def per_device(output_gate, input_gate, values_in, filters, cotangent):
    seq_count = lax.axis_size("seq")
    chan_count = lax.axis_size("ch")
    per_group = seq_count // chan_count
    length, owned = filters.shape
    scale = 1.0 / math.sqrt(length)
    swap = []
    for s in range(seq_count):
        for c in range(chan_count):
            high, low = divmod(s, per_group)
            swap.append((s * chan_count + c, (c * per_group + low) * chan_count + high))
    tables = {name: jnp.asarray(table) for name, table in dft_tables(seq_count).items()}
    filters_here = lax.ppermute(filters.T, ("seq", "ch"), swap)
    filter_spectrum = filter_spectra(filters_here, tables)
    send = gates(output_gate, input_gate, values_in, cotangent, seq_count, chan_count)
    sections = send.reshape(seq_count, 2, owned, LANES)
    received = lax.all_to_all(sections, "seq", split_axis=0, concat_axis=0, tiled=True)
    back, own_spectrum, sizes = convolutions(received, filter_spectrum, tables, scale)
    grads = filter_gradients(own_spectrum, sizes, seq_count, tables, scale)
    grads_owned = lax.ppermute(grads, ("seq", "ch"), swap)
    returned = lax.all_to_all(back, "seq", split_axis=0, concat_axis=0, tiled=True)
    returned = returned.reshape(chan_count, per_group, 2, owned, LANES)
    grad_filters = filter_results(grads_owned).T
    output, grad_out, grad_in, grad_values = results(
        output_gate, input_gate, values_in, cotangent, returned
    )
    return (output, grad_out, grad_in, grad_values, grad_filters)


def solution(mesh):
    by_position = P("seq", "ch")
    by_channel = P(None, ("seq", "ch"))
    return jax.shard_map(
        per_device,
        mesh=mesh,
        in_specs=(by_position, by_position, by_position, by_channel, by_position),
        out_specs=(by_position, by_position, by_position, by_position, by_channel),
        check_vma=False,
    )
```

time: 159 us -> 97.1 us (0.61)
  Pallas kernels: 87.5 us -> 24.8 us
  local copies, waits for them, and re-layouts: 1.5 us -> 8.79 us
  waiting for transfers between devices: 33.7 us -> 27 us
    pallas_call x1 -> x3, Pallas kernels: 77.9 us -> 15.1 us  [the longest x1 7.64 us: convolutions(): pl.pallas_call(functools.partial(convolution_kernel, scale / (LANES * LAN...]
    unnamed x6 -> x28, local copies, waits for them, and re-layouts: 1.5 us -> 8.79 us
    ppermute x1, waiting for transfers between devices: 16 us -> 9.27 us  [per_device(): grads_owned = lax.ppermute(grads, ('seq', 'ch'), swap)]
  transfers between devices with their start and end apart: 4 -> 4, of which waited for: 2 -> 2; matrix products, arithmetic and copies ran while one was open for 0% -> 0% of each run, Pallas kernels for 1% -> 10%
where the time goes in v1:
time: 97.1 us; the launch traced here: 96.4 us
  starting transfers between devices  35 us (36%)
  waiting for transfers between devices  27 us (28%)
  Pallas kernels  24.8 us (26%)
  local copies, waits for them, and re-layouts  8.79 us (9%)
    ppermute x1, waiting for transfers between devices, per_device(): filters_here = lax.ppermute(filters.T, ('seq', 'ch'), swap)  17.7 us
    all_to_all x1, starting transfers between devices, per_device(): lax.all_to_all(sections, 'seq', split_axis=0, concat_axis=0, tiled=True)  13.8 us
    ppermute x1, waiting for transfers between devices, per_device(): grads_owned = lax.ppermute(grads, ('seq', 'ch'), swap)  9.27 us
    unnamed x28, local copies, waits for them, and re-layouts  8.79 us
    all_to_all x1, starting transfers between devices, per_device(): lax.all_to_all(back, 'seq', split_axis=0, concat_axis=0, tiled=True)  7.73 us
    pallas_call x1, Pallas kernels, convolutions(): pl.pallas_call(functools.partial(convolution_kernel, scale / (LANES * LAN...  7.64 us
    ppermute x1, starting transfers between devices, per_device(): filters_here = lax.ppermute(filters.T, ('seq', 'ch'), swap)  7.03 us
    ppermute x1, starting transfers between devices, per_device(): grads_owned = lax.ppermute(grads, ('seq', 'ch'), swap)  6.46 us
  transfers between devices with their start and end apart: 4, of which 2 were waited for; matrix products, arithmetic and copies ran while one was open for 0% of the time, Pallas kernels for 10%

profile of v1, /device:TPU:32, one launch (start us, length us, event | category | flops | bytes accessed | tf_op | source)
XLA Modules:
  0.0 96.4 jit_solution(16868965806822632135)
XLA Ops:
  0.6 0.0 copy-start.4
  0.6 0.0 copy-start.5
  0.7 0.0 copy-start.3
  0.7 3.8 %gate_products.1 = bf16[4,16,2,16,128]{4,3,2,1,0:T(8,128)(2,1)} custom-call(bf16[128,1024]{1,0:T(8,128)(2,1)} %out_gate.3, bf16[128,1024]{1,0:T(8,128)(2,1)} %in_gate.3, bf16[128,1024]{1,0:T(8,128)(2,1)} %values.3, bf16[128,1024]{1,0:T(8,128)(2,1)} %cotan.3), custom_call_target="tpu_custom_call" | custom-call | tf_op jit(solution)/shard_map/gate_products/pallas_call | solution.py:42
  4.5 13.8 %all-to-all-start = ((bf16[64,2,16,128]{3,2,1,0:T(8,128)(2,1)}), bf16[64,2,16,128]{3,2,1,0:T(8,128)(2,1)S(1)}, u32[]{:S(2)}, u32[]{:S(2)}) async-start(bf16[64,2,16,128]{3,2,1,0:T(8,128)(2,1)} %bitcast.5), calls=%async_computation | async-start | bytes 1048576 | tf_op jit(solution)/shard_map/all_to_all | solution.py:387
  18.3 7.0 %collective-permute-start = (bf16[16,8192]{1,0:T(8,128)(2,1)S(1)}, bf16[16,8192]{1,0:T(8,128)(2,1)S(1)}, u32[]{:S(2)}, u32[]{:S(2)}) collective-permute-start(bf16[16,8192]{1,0:T(8,128)(2,1)S(1)} %bitcast.7), channel_id=1, source_target_pairs={{0,0},{1,64},{2,128},{3,192},{4,4},{5,68},{6,132},{7,196},{8,8},{9... | collective-permute-start | bytes 786440 | tf_op jit(solution)/shard_map/ppermute | solution.py:383
  25.4 17.7 %collective-permute-done.filters = bf16[16,8192]{1,0:T(8,128)(2,1)S(1)} collective-permute-done((bf16[16,8192]{1,0:T(8,128)(2,1)S(1)}, bf16[16,8192]{1,0:T(8,128)(2,1)S(1)}, u32[]{:S(2)}, u32[]{:S(2)}) %collective-permute-start) | collective-permute-done | bytes 262176 | tf_op jit(solution)/shard_map/ppermute | solution.py:383
  43.1 0.8 copy-done.10
  43.9 3.2 %filter_spectra.1.filter_spectrum = f32[16,128,256]{2,1,0:T(8,128)S(1)} custom-call(bf16[16,8192]{1,0:T(8,128)(2,1)S(1)} %collective-permute-done.filters, bf16[256,128]{1,0:T(8,128)(2,1)S(1)} %copy-done.10, bf16[768,256]{1,0:T(8,128)(2,1)S(1)} %copy-done.3, f32[128,128]{1,0:T(8,128)S(1)} %copy-done.5, f32[128,128]{1,0:T(8,128)S(1)} %copy-done.4), custom_call_target="tpu_custom_call" | custom-call | tf_op jit(solution)/shard_map/filter_spectra/pallas_call | solution.py:260
  47.2 0.9 copy-done.7
  48.1 0.9 copy-done.8
  49.0 7.6 %convolutions.1 = (bf16[64,2,16,128]{3,2,1,0:T(8,128)(2,1)S(1)}, f32[16,128,256]{2,1,0:T(8,128)S(1)}, f32[2,16,128]{2,1,0:T(8,128)S(1)}) custom-call(bf16[64,2,16,128]{3,2,1,0:T(8,128)(2,1)S(1)} %all-to-all-done.received, f32[16,128,256]{2,1,0:T(8,128)S(1)} %filter_spectra.1.filter_spectrum, bf16[256,256]{1,0:T(8,128)(2,1)S(1)} %copy-done.8, ...), custom_call_target="tpu_custom_call" | custom-call | tf_op jit(solution)/shard_map/convolutions/pallas_call | solution.py:273
  56.6 1.3 %copy-done = f32[16,128,256]{2,1,0:T(8,128)} copy-done((f32[16,128,256]{2,1,0:T(8,128)}, f32[16,128,256]{2,1,0:T(8,128)S(1)}, u32[]{:S(2)}) %copy-start) | copy-done | bytes 2097176
  58.0 0.8 copy-done.6
  58.8 7.7 %all-to-all-start.1 = ((bf16[64,2,16,128]{3,2,1,0:T(8,128)(2,1)}), bf16[64,2,16,128]{3,2,1,0:T(8,128)(2,1)S(1)}, u32[]{:S(2)}, u32[]{:S(2)}) async-start(bf16[64,2,16,128]{3,2,1,0:T(8,128)(2,1)} %copy-done.6), calls=%async_computation.1 | async-start | bytes 1048576 | tf_op jit(solution)/shard_map/all_to_all | solution.py:391
  66.5 1.6 %copy-done.1 = f32[16,128,256]{2,1,0:T(8,128)S(1)} copy-done((f32[16,128,256]{2,1,0:T(8,128)S(1)}, f32[16,128,256]{2,1,0:T(8,128)}, u32[]{:S(2)}) %copy-start.1) | copy-done | bytes 2097176
  68.1 0.9 copy-done.9
  69.0 4.3 %filter_gradients.1 = bf16[64,16,128]{2,1,0:T(8,128)(2,1)S(1)} custom-call(f32[16,128,256]{2,1,0:T(8,128)S(1)} %copy-done.1, f32[2,16,128]{2,1,0:T(8,128)S(1)} %get-tuple-element.18.sizes, bf16[64,768]{1,0:T(8,128)(2,1)S(1)} %copy-done.9, bf16[768,256]{1,0:T(8,128)(2,1)S(1)} %copy-done.2, f32[128,128]{1,0:T(8,128)S(1)} %copy-done.5, f32[128,128]{1,0:T(8,128)S(1)} %copy-done.4), custom_call_target="tpu_custom_call" | custom-call | tf_op jit(solution)/shard_map/filter_gradients/pallas_call | solution.py:302
  73.3 6.5 %collective-permute-start.1 = (bf16[64,16,128]{2,1,0:T(8,128)(2,1)S(1)}, bf16[64,16,128]{2,1,0:T(8,128)(2,1)S(1)}, u32[]{:S(2)}, u32[]{:S(2)}) collective-permute-start(bf16[64,16,128]{2,1,0:T(8,128)(2,1)S(1)} %filter_gradients.1), channel_id=1, source_target_pairs={{0,0},{1,64},{2,128},{3,192},{4,4},{5,68},{6,132},{7,196},{8,8},{9... | collective-permute-start | bytes 786440 | tf_op jit(solution)/shard_map/ppermute | solution.py:390
  79.8 9.3 %collective-permute-done.1.received = bf16[64,16,128]{2,1,0:T(8,128)(2,1)S(1)} collective-permute-done((bf16[64,16,128]{2,1,0:T(8,128)(2,1)S(1)}, bf16[64,16,128]{2,1,0:T(8,128)(2,1)S(1)}, u32[]{:S(2)}, u32[]{:S(2)}) %collective-permute-start.1) | collective-permute-done | bytes 262176 | tf_op jit(solution)/shard_map/ppermute | solution.py:390
  89.0 0.7 copy-done.12
  89.7 2.0 %filter_results.1 = f32[16,8192]{1,0:T(8,128)} custom-call(bf16[64,16,128]{2,1,0:T(8,128)(2,1)} %copy-done.12), custom_call_target="tpu_custom_call" | custom-call | tf_op jit(solution)/shard_map/filter_results/pallas_call | solution.py:364
  91.7 0.8 copy-done.11
  92.5 3.9 %gate_results.1 = (bf16[128,1024]{1,0:T(8,128)(2,1)}, bf16[128,1024]{1,0:T(8,128)(2,1)}, bf16[128,1024]{1,0:T(8,128)(2,1)}, bf16[128,1024]{1,0:T(8,128)(2,1)}) custom-call(bf16[128,1024]{1,0:T(8,128)(2,1)} %out_gate.3, bf16[128,1024]{1,0:T(8,128)(2,1)} %in_gate.3, bf16[128,1024]{1,0:T(8,128)(2,1)} %values.3, bf16[128,1024]{1,0:T(8,128)(2,1)} %cotan.3, ...), custom_call_target="tpu_custom_call" | custom-call | tf_op jit(solution)/shard_map/gate_results/pallas_call | solution.py:342
  (18 shorter events, 0.0 us)
Async XLA Ops:
  0.6 42.4 %copy-start.4 = (f32[128,128]{1,0:T(8,128)S(1)}, f32[128,128]{1,0:T(8,128)}, u32[]{:S(2)}) copy-start(f32[128,128]{1,0:T(8,128)} %constant.23.clone.turn_sin) | copy-start | bytes 196612
  0.6 42.4 %copy-start.5 = (f32[128,128]{1,0:T(8,128)S(1)}, f32[128,128]{1,0:T(8,128)}, u32[]{:S(2)}) copy-start(f32[128,128]{1,0:T(8,128)} %constant.22.clone.turn_cos) | copy-start | bytes 196612
  0.7 42.4 %copy-start.3 = (bf16[768,256]{1,0:T(8,128)(2,1)S(1)}, bf16[768,256]{1,0:T(8,128)(2,1)}, u32[]{:S(2)}) copy-start(bf16[768,256]{1,0:T(8,128)(2,1)} %constant.18.clone.second) | copy-start | bytes 1179652
  0.7 17.7 %copy-start.13 = (bf16[8192,16]{0,1:T(8,128)(2,1)S(1)}, bf16[8192,16]{0,1:T(8,128)(2,1)}, u32[]{:S(2)}) copy-start(bf16[8192,16]{0,1:T(8,128)(2,1)} %param.16) | copy-start | bytes 786436
  4.5 42.6 %copy-start.2 = (bf16[768,256]{1,0:T(8,128)(2,1)S(1)}, bf16[768,256]{1,0:T(8,128)(2,1)}, u32[]{:S(2)}) copy-start(bf16[768,256]{1,0:T(8,128)(2,1)} %constant.19.clone.second_back) | copy-start | bytes 1179652
  4.5 42.6 %all-to-all-start = ((bf16[64,2,16,128]{3,2,1,0:T(8,128)(2,1)}), bf16[64,2,16,128]{3,2,1,0:T(8,128)(2,1)S(1)}, u32[]{:S(2)}, u32[]{:S(2)}) async-start(bf16[64,2,16,128]{3,2,1,0:T(8,128)(2,1)} %bitcast.5), calls=%async_computation | async-start | bytes 1048576 | tf_op jit(solution)/shard_map/all_to_all | solution.py:387
  18.3 24.7 %collective-permute-start = (bf16[16,8192]{1,0:T(8,128)(2,1)S(1)}, bf16[16,8192]{1,0:T(8,128)(2,1)S(1)}, u32[]{:S(2)}, u32[]{:S(2)}) collective-permute-start(bf16[16,8192]{1,0:T(8,128)(2,1)S(1)} %bitcast.7), channel_id=1, source_target_pairs={{0,0},{1,64},{2,128},{3,192},{4,4},{5,68},{6,132},{7,196},{8,8},{9... | collective-permute-start | bytes 786440 | tf_op jit(solution)/shard_map/ppermute | solution.py:383
  43.1 0.8 copy-start.10
  47.2 0.9 copy-start.7
  48.1 0.9 copy-start.8
  56.6 1.3 %copy-start = (f32[16,128,256]{2,1,0:T(8,128)}, f32[16,128,256]{2,1,0:T(8,128)S(1)}, u32[]{:S(2)}) copy-start(f32[16,128,256]{2,1,0:T(8,128)S(1)} %get-tuple-element.17.own_spectrum) | copy-start | bytes 6291460
  58.0 0.8 copy-start.6
  58.8 32.9 %all-to-all-start.1 = ((bf16[64,2,16,128]{3,2,1,0:T(8,128)(2,1)}), bf16[64,2,16,128]{3,2,1,0:T(8,128)(2,1)S(1)}, u32[]{:S(2)}, u32[]{:S(2)}) async-start(bf16[64,2,16,128]{3,2,1,0:T(8,128)(2,1)} %copy-done.6), calls=%async_computation.1 | async-start | bytes 1048576 | tf_op jit(solution)/shard_map/all_to_all | solution.py:391
  66.5 1.6 %copy-start.1 = (f32[16,128,256]{2,1,0:T(8,128)S(1)}, f32[16,128,256]{2,1,0:T(8,128)}, u32[]{:S(2)}) copy-start(f32[16,128,256]{2,1,0:T(8,128)} %copy-done) | copy-start | bytes 6291460
  68.1 0.9 copy-start.9
  73.3 15.7 %collective-permute-start.1 = (bf16[64,16,128]{2,1,0:T(8,128)(2,1)S(1)}, bf16[64,16,128]{2,1,0:T(8,128)(2,1)S(1)}, u32[]{:S(2)}, u32[]{:S(2)}) collective-permute-start(bf16[64,16,128]{2,1,0:T(8,128)(2,1)S(1)} %filter_gradients.1), channel_id=1, source_target_pairs={{0,0},{1,64},{2,128},{3,192},{4,4},{5,68},{6,132},{7,196},{8,8},{9... | collective-permute-start | bytes 786440 | tf_op jit(solution)/shard_map/ppermute | solution.py:390
  89.0 0.7 copy-start.12
  91.7 0.8 copy-start.11

commit v2 on v1

--- a/solution.py
+++ b/solution.py
@@ -25,9 +25,9 @@
     groups, per_group, _, owned, _ = send.shape
     mixed = (in_gate[...].astype(WIDE) * values[...].astype(WIDE)).astype(NARROW)
     gated = (cotan[...].astype(WIDE) * out_gate[...].astype(WIDE)).astype(NARROW)
-    flipped = jnp.dot(exchange_matrix(), gated, preferred_element_type=WIDE)
-    for which, array in enumerate((mixed.astype(WIDE), flipped)):
-        turned = array.T.astype(NARROW).reshape(per_group, groups, owned, LANES)
+    flipped = dot(gated.T, exchange_matrix()).astype(NARROW)
+    for which, array in enumerate((mixed.T, flipped)):
+        turned = array.reshape(per_group, groups, owned, LANES)
         for g in range(groups):
             send[g, :, which] = turned[:, g]
 
@@ -37,7 +37,7 @@
     groups = chan_count
     per_group = seq_count // chan_count
     owned = width // seq_count
-    steps = 4
+    steps = 2
     block = pl.BlockSpec((LANES, width // steps), lambda i: (0, i))
     return pl.pallas_call(
         gate_kernel,
@@ -45,6 +45,7 @@
         in_specs=[block] * 4,
         out_specs=pl.BlockSpec((groups, per_group // steps, 2, owned, LANES), lambda i: (0, i, 0, 0, 0)),
         out_shape=jax.ShapeDtypeStruct((groups, per_group, 2, owned, LANES), NARROW),
+        cost_estimate=cost(2),
         name="gate_products",
     )(out_gate, in_gate, values, cotan)
 
@@ -157,6 +158,17 @@
 
 def convolution_kernel(
     scale,
+    received_far,
+    spectrum_far,
+    first_far,
+    second_far,
+    first_back_far,
+    second_back_far,
+    turn_cos_far,
+    turn_sin_far,
+    first_back_imag_far,
+    send_far,
+    grad_filters,
     received,
     filter_spectrum,
     first,
@@ -165,23 +177,57 @@
     second_back,
     turn_cos,
     turn_sin,
+    first_back_imag,
     send,
-    own_spectrum,
-    sizes,
     signal,
     back,
+    grads,
+    loaded,
+    sent,
 ):
     blocks, _, owned, _ = received.shape
+    far = (
+        received_far,
+        first_far,
+        turn_cos_far,
+        turn_sin_far,
+        second_far,
+        spectrum_far,
+        second_back_far,
+        first_back_far,
+        first_back_imag_far,
+    )
+    near = (
+        received,
+        first,
+        turn_cos,
+        turn_sin,
+        second,
+        filter_spectrum,
+        second_back,
+        first_back,
+        first_back_imag,
+    )
+    loads = [
+        pltpu.make_async_copy(one, other, loaded.at[at])
+        for at, (one, other) in enumerate(zip(far, near))
+    ]
+    for load in loads:
+        load.start()
+    loads[0].wait()
+    ups = []
     for which in range(2):
         size = jnp.zeros((owned, LANES), WIDE)
         for j in range(blocks):
             size = jnp.maximum(size, jnp.abs(received[j, which].astype(WIDE)))
         size = jnp.broadcast_to(jnp.max(size, axis=1, keepdims=True), (owned, LANES))
         down, up = power_of_two(size)
-        sizes[which] = up
+        ups.append(up)
         for j in range(blocks):
             at = j if which == 0 else blocks - 1 - j
             signal[which, pl.ds(at * owned, owned), :] = received[j, which].astype(WIDE) * down
+    for load in loads[1:]:
+        load.wait()
 
     def pair(at, carry):
         data = []
@@ -193,9 +239,10 @@
             data.append(jnp.concatenate(rows, axis=0))
         found = spectra(data, first, second, turn_cos, turn_sin)
         products = []
+        squares = []
         for c in range(TOGETHER):
-            own_spectrum[TOGETHER * at + c] = found[c]
             real, imag = found[c][:, :LANES], found[c][:, LANES:]
+            squares.append((0.5 * (real - imag) * (real + imag), real * imag))
             taps_real = filter_spectrum[TOGETHER * at + c, :, :LANES]
             taps_imag = filter_spectrum[TOGETHER * at + c, :, LANES:]
             products.append(
@@ -207,52 +254,42 @@
                 back[which, pl.ds(TOGETHER * at + c, blocks, stride=owned), :] = result[c][
                     which * blocks : (which + 1) * blocks
                 ]
-        return carry
-
-    lax.fori_loop(0, owned // TOGETHER, pair, 0)
-    for which in range(2):
-        up = sizes[which] * scale
-        for j in range(blocks):
-            at = j if which == 0 else blocks - 1 - j
-            send[at, which] = (back[which, pl.ds(j * owned, owned), :] * up).astype(NARROW)
-
-
-def gradient_kernel(
-    scale,
-    own_spectrum,
-    sizes,
-    first_back_imag,
-    second_back,
-    turn_cos,
-    turn_sin,
-    grad_filters,
-    grads,
-):
-    blocks, owned, _ = grad_filters.shape
-
-    def pair(at, carry):
-        squares = []
-        for c in range(TOGETHER):
-            real = own_spectrum[TOGETHER * at + c, :, :LANES]
-            imag = own_spectrum[TOGETHER * at + c, :, LANES:]
-            squares.append((0.5 * (real - imag) * (real + imag), real * imag))
         result = signals(squares, first_back_imag, second_back, turn_cos, turn_sin)
         for c in range(TOGETHER):
             grads[pl.ds(TOGETHER * at + c, blocks, stride=owned), :] = result[c]
         return carry
 
     lax.fori_loop(0, owned // TOGETHER, pair, 0)
-    up = sizes[0] * sizes[1] * scale
+    up = ups[0] * ups[1] * scale
     for j in range(blocks):
         grad_filters[j] = (grads[pl.ds(j * owned, owned), :] * up).astype(NARROW)
+    up = [one * scale for one in ups]
+    pieces = 4
+    rows = blocks // pieces
+    sends = []
+    for piece in range(pieces):
+        for at in range(piece * rows, (piece + 1) * rows):
+            for which in range(2):
+                j = at if which == 0 else blocks - 1 - at
+                value = back[which, pl.ds(j * owned, owned), :] * up[which]
+                send[at, which] = value.astype(NARROW)
+        part = pl.ds(piece * rows, rows)
+        sends.append(pltpu.make_async_copy(send.at[part], send_far.at[part], sent.at[piece]))
+        sends[-1].start()
+    for one in sends:
+        one.wait()
 
 
 def in_vmem(count):
     return [pl.BlockSpec(memory_space=pltpu.VMEM)] * count
 
 
-def params():
-    return pltpu.CompilerParams(vmem_limit_bytes=32 * 1024 * 1024)
+def params(mebibytes=60):
+    return pltpu.CompilerParams(vmem_limit_bytes=mebibytes * 1024 * 1024)
+
+
+def cost(micros):
+    return pl.CostEstimate(flops=int(micros * 1e9), bytes_accessed=1024, transcendentals=0)
 
 
 def filter_spectra(filters, tables):
@@ -264,28 +301,14 @@
         out_shape=jax.ShapeDtypeStruct((owned, LANES, 2 * LANES), WIDE),
         scratch_shapes=[pltpu.VMEM((length // LANES * owned, LANES), WIDE)],
         compiler_params=params(),
+        cost_estimate=cost(12),
         name="filter_spectra",
     )(filters, tables["first_real"], tables["second"], tables["turn_cos"], tables["turn_sin"])
 
 
 def convolutions(received, filter_spectrum, tables, scale):
     blocks, _, owned, _ = received.shape
-    return pl.pallas_call(
-        functools.partial(convolution_kernel, scale / (LANES * LANES)),
-        in_specs=in_vmem(8),
-        out_specs=in_vmem(3),
-        out_shape=[
-            jax.ShapeDtypeStruct(received.shape, NARROW),
-            jax.ShapeDtypeStruct((owned, LANES, 2 * LANES), WIDE),
-            jax.ShapeDtypeStruct((2, owned, LANES), WIDE),
-        ],
-        scratch_shapes=[
-            pltpu.VMEM((2, blocks * owned, LANES), WIDE),
-            pltpu.VMEM((2, blocks * owned, LANES), WIDE),
-        ],
-        compiler_params=params(),
-        name="convolutions",
-    )(
+    operands = (
         received,
         filter_spectrum,
         tables["first"],
@@ -294,27 +317,30 @@
         tables["second_back"],
         tables["turn_cos"],
         tables["turn_sin"],
-    )
-
-
-def filter_gradients(own_spectrum, sizes, blocks, tables, scale):
-    owned = own_spectrum.shape[0]
+        tables["first_back_imag"],
+    )
+    far = pl.BlockSpec(memory_space=pl.ANY)
     return pl.pallas_call(
-        functools.partial(gradient_kernel, scale / (LANES * LANES)),
-        in_specs=in_vmem(6),
-        out_specs=in_vmem(1)[0],
-        out_shape=jax.ShapeDtypeStruct((blocks, owned, LANES), NARROW),
-        scratch_shapes=[pltpu.VMEM((blocks * owned, LANES), WIDE)],
-        compiler_params=params(),
-        name="filter_gradients",
-    )(
-        own_spectrum,
-        sizes,
-        tables["first_back_imag"],
-        tables["second_back"],
-        tables["turn_cos"],
-        tables["turn_sin"],
-    )
+        functools.partial(convolution_kernel, scale / (LANES * LANES)),
+        in_specs=[far] * len(operands),
+        out_specs=[far] + in_vmem(1),
+        out_shape=[
+            jax.ShapeDtypeStruct(received.shape, NARROW),
+            jax.ShapeDtypeStruct((blocks, owned, LANES), NARROW),
+        ],
+        scratch_shapes=[pltpu.VMEM(one.shape, one.dtype) for one in operands]
+        + [
+            pltpu.VMEM(received.shape, NARROW),
+            pltpu.VMEM((2, blocks * owned, LANES), WIDE),
+            pltpu.VMEM((2, blocks * owned, LANES), WIDE),
+            pltpu.VMEM((blocks * owned, LANES), WIDE),
+            pltpu.SemaphoreType.DMA((len(operands),)),
+            pltpu.SemaphoreType.DMA((4,)),
+        ],
+        compiler_params=params(48),
+        cost_estimate=cost(6),
+        name="convolutions",
+    )(*operands)
 
 
 def result_kernel(out_gate, in_gate, values, cotan, received, output, grad_out, grad_in, grad_values):
@@ -322,12 +348,9 @@
     turned = []
     for which in range(2):
         pieces = [received[g, :, which] for g in range(groups)]
-        array = jnp.stack(pieces, axis=1).reshape(groups * per_group * owned, LANES)
-        turned.append(array.astype(WIDE).T)
-    conv = turned[0]
-    grad_mixed = jnp.dot(
-        exchange_matrix(), turned[1].astype(NARROW), preferred_element_type=WIDE
-    )
+        turned.append(jnp.stack(pieces, axis=1).reshape(groups * per_group * owned, LANES))
+    conv = turned[0].T.astype(WIDE)
+    grad_mixed = dot(turned[1], exchange_matrix()).astype(NARROW).T.astype(WIDE)
     output[...] = (out_gate[...].astype(WIDE) * conv).astype(NARROW)
     grad_out[...] = (cotan[...].astype(WIDE) * conv).astype(NARROW)
     grad_in[...] = (grad_mixed * values[...].astype(WIDE)).astype(NARROW)
@@ -337,7 +360,7 @@
 def results(out_gate, in_gate, values, cotan, received):
     groups, per_group, _, owned, _ = received.shape
     width = out_gate.shape[1]
-    steps = 4
+    steps = 2
     block = pl.BlockSpec((LANES, width // steps), lambda i: (0, i))
     return pl.pallas_call(
         result_kernel,
@@ -346,6 +369,8 @@
         + [pl.BlockSpec((groups, per_group // steps, 2, owned, LANES), lambda i: (0, i, 0, 0, 0))],
         out_specs=[block] * 4,
         out_shape=[jax.ShapeDtypeStruct(out_gate.shape, NARROW)] * 4,
+        compiler_params=params(48),
+        cost_estimate=cost(2),
         name="gate_results",
     )(out_gate, in_gate, values, cotan, received)
 
@@ -353,8 +378,7 @@
 def filter_kernel(received, grad_filters):
     blocks, owned, _ = received.shape
     flat = received[...].reshape(blocks * owned, LANES)
-    flipped = jnp.dot(flat, exchange_matrix(), preferred_element_type=WIDE)
-    flipped = flipped.reshape(blocks, owned, LANES)
+    flipped = dot(flat, exchange_matrix()).reshape(blocks, owned, LANES)
     for j in range(blocks):
         grad_filters[:, pl.ds(j * LANES, LANES)] = flipped[blocks - 1 - j]
 
@@ -364,6 +388,8 @@
     return pl.pallas_call(
         filter_kernel,
         out_shape=jax.ShapeDtypeStruct((owned, blocks * LANES), WIDE),
+        compiler_params=params(48),
+        cost_estimate=cost(12),
         name="filter_results",
     )(received)
 
@@ -385,8 +411,7 @@
     send = gates(output_gate, input_gate, values_in, cotangent, seq_count, chan_count)
     sections = send.reshape(seq_count, 2, owned, LANES)
     received = lax.all_to_all(sections, "seq", split_axis=0, concat_axis=0, tiled=True)
-    back, own_spectrum, sizes = convolutions(received, filter_spectrum, tables, scale)
-    grads = filter_gradients(own_spectrum, sizes, seq_count, tables, scale)
+    back, grads = convolutions(received, filter_spectrum, tables, scale)
     grads_owned = lax.ppermute(grads, ("seq", "ch"), swap)
     returned = lax.all_to_all(back, "seq", split_axis=0, concat_axis=0, tiled=True)
     returned = returned.reshape(chan_count, per_group, 2, owned, LANES)

time: 97.1 us -> 84.1 us (0.87)
  the two profiles are of different devices: /device:TPU:32 before, /device:TPU:2 now
where the time goes in v2:
time: 84.1 us; the launch traced here: 83.8 us
  waiting for transfers between devices  29.7 us (35%)
  starting transfers between devices  28.2 us (34%)
  Pallas kernels  22.8 us (27%)
  local copies, waits for them, and re-layouts  2.35 us (3%)
    all_to_all x1, waiting for transfers between devices, per_device(): lax.all_to_all(back, 'seq', split_axis=0, concat_axis=0, tiled=True)  16.1 us
    all_to_all x1, starting transfers between devices, per_device(): lax.all_to_all(sections, 'seq', split_axis=0, concat_axis=0, tiled=True)  15 us
    all_to_all x1, waiting for transfers between devices, per_device(): lax.all_to_all(sections, 'seq', split_axis=0, concat_axis=0, tiled=True)  13.6 us
    pallas_call x1, Pallas kernels, convolutions(): pl.pallas_call(functools.partial(convolution_kernel, scale / (LANES * LAN...  12.3 us
    all_to_all x1, starting transfers between devices, per_device(): lax.all_to_all(back, 'seq', split_axis=0, concat_axis=0, tiled=True)  10.9 us
    pallas_call x1, Pallas kernels, filter_spectra(): pl.pallas_call(spectrum_kernel, in_specs=in_vmem(5), out_specs=in_vmem(1)...  5.69 us
    unnamed x26, local copies, waits for them, and re-layouts  2.35 us
    pallas_call x1, Pallas kernels, gates(): pl.pallas_call(gate_kernel, grid=(steps,), in_specs=[block] * 4, out_spec...  2.27 us
  transfers between devices with their start and end apart: 4, of which 2 were waited for; matrix products, arithmetic and copies ran while one was open for 0% of the time, Pallas kernels for 11%

profile of v2, /device:TPU:2, one launch (start us, length us, event | category | flops | bytes accessed | tf_op | source)
XLA Modules:
  0.0 83.8 jit_solution(12049189985232411014)
XLA Ops:
  0.6 1.6 %collective-permute-start = (bf16[16,8192]{1,0:T(8,128)(2,1)}, bf16[16,8192]{1,0:T(8,128)(2,1)S(1)}, u32[]{:S(2)}, u32[]{:S(2)}) collective-permute-start(bf16[16,8192]{1,0:T(8,128)(2,1)} %bitcast.6), channel_id=1, source_target_pairs={{0,0},{1,64},{2,128},{3,192},{4,4},{5,68},{6,132},{7,196},{8,8},{9... | collective-permute-start | bytes 786440 | tf_op jit(solution)/shard_map/ppermute | solution.py:409
  2.2 2.3 %gate_products.1 = bf16[4,16,2,16,128]{4,3,2,1,0:T(8,128)(2,1)} custom-call(bf16[128,1024]{1,0:T(8,128)(2,1)} %out_gate.3, bf16[128,1024]{1,0:T(8,128)(2,1)} %in_gate.3, bf16[128,1024]{1,0:T(8,128)(2,1)} %values.3, bf16[128,1024]{1,0:T(8,128)(2,1)} %cotan.3), custom_call_target="tpu_custom_call" | custom-call | flops 2000000000 | bytes 1024 | tf_op jit(solution)/shard_map/gate_products/pallas_call | solution.py:42
  4.5 15.0 %all-to-all-start = ((bf16[64,2,16,128]{3,2,1,0:T(8,128)(2,1)}), bf16[64,2,16,128]{3,2,1,0:T(8,128)(2,1)S(1)}, u32[]{:S(2)}, u32[]{:S(2)}) async-start(bf16[64,2,16,128]{3,2,1,0:T(8,128)(2,1)} %bitcast.5), calls=%async_computation | async-start | bytes 1048576 | tf_op jit(solution)/shard_map/all_to_all | solution.py:413
  19.5 0.0 copy-start.4
  19.5 0.0 copy-start.5
  19.5 0.0 copy-start.6
  19.5 0.0 copy-start.7
  19.6 0.0 copy-start.8
  19.6 0.0 copy-start.9
  19.6 0.0 copy-start.10
  19.6 0.0 copy-start.12
  19.6 0.7 copy-done.12
  20.3 5.7 %filter_spectra.1.spectrum_far = f32[16,128,256]{2,1,0:T(8,128)} custom-call(bf16[16,8192]{1,0:T(8,128)(2,1)} %copy-done.12, bf16[256,128]{1,0:T(8,128)(2,1)} %constant.17.clone.first, bf16[768,256]{1,0:T(8,128)(2,1)} %constant.18.clone.second.second_far, f32[128,128]{1,0:T(8,128)} %constant.22.clone.turn_cos.turn_cos_far, ...), custom_call_target="tpu_custom_call" | custom-call | flops 12000000000 | bytes 1024 | tf_op jit(solution)/shard_map/filter_spectra/pallas_call | solution.py:297
  26.0 13.6 %all-to-all-done.received_far = bf16[64,2,16,128]{3,2,1,0:T(8,128)(2,1)S(1)} async-done(((bf16[64,2,16,128]{3,2,1,0:T(8,128)(2,1)}), bf16[64,2,16,128]{3,2,1,0:T(8,128)(2,1)S(1)}, u32[]{:S(2)}, u32[]{:S(2)}) %all-to-all-start) | async-done | bytes 524320 | tf_op jit(solution)/shard_map/all_to_all | solution.py:413
  39.6 1.6 %copy-done.11 = f32[16,128,256]{2,1,0:T(8,128)S(1)} copy-done((f32[16,128,256]{2,1,0:T(8,128)S(1)}, f32[16,128,256]{2,1,0:T(8,128)}, u32[]{:S(2)}) %copy-start.11) | copy-done | bytes 2097176
  41.2 12.3 %convolutions.1 = (bf16[64,2,16,128]{3,2,1,0:T(8,128)(2,1)}, bf16[64,16,128]{2,1,0:T(8,128)(2,1)S(1)}) custom-call(bf16[64,2,16,128]{3,2,1,0:T(8,128)(2,1)S(1)} %all-to-all-done.received_far, f32[16,128,256]{2,1,0:T(8,128)S(1)} %copy-done.11, bf16[256,256]{1,0:T(8,128)(2,1)S(1)} %copy-done.7, bf16[768,256]{1,0:T(8,128)(2,1)S(1)} %copy-done.4, ...), custom_call_target="tpu_custom_call" | custom-call | flops 6000000000 | bytes 1024 | tf_op jit(solution)/shard_map/convolutions/pallas_call | solution.py:323
  53.6 0.7 collective-permute-start.1
  54.2 10.9 %all-to-all-start.1 = ((bf16[64,2,16,128]{3,2,1,0:T(8,128)(2,1)}), bf16[64,2,16,128]{3,2,1,0:T(8,128)(2,1)S(1)}, u32[]{:S(2)}, u32[]{:S(2)}) async-start(bf16[64,2,16,128]{3,2,1,0:T(8,128)(2,1)} %get-tuple-element.11), calls=%async_computation.1 | async-start | bytes 1048576 | tf_op jit(solution)/shard_map/all_to_all | solution.py:416
  65.2 0.0 copy-start
  65.2 0.0 copy-start.1
  65.2 0.0 copy-start.2
  65.2 1.0 %filter_results.1 = f32[16,8192]{1,0:T(8,128)} custom-call(bf16[64,16,128]{2,1,0:T(8,128)(2,1)S(1)} %collective-permute-done.1.received), custom_call_target="tpu_custom_call" | custom-call | flops 12000000000 | bytes 1024 | tf_op jit(solution)/shard_map/filter_results/pallas_call | solution.py:388
  66.2 16.1 %all-to-all-done.1 = bf16[64,2,16,128]{3,2,1,0:T(8,128)(2,1)S(1)} async-done(((bf16[64,2,16,128]{3,2,1,0:T(8,128)(2,1)}), bf16[64,2,16,128]{3,2,1,0:T(8,128)(2,1)S(1)}, u32[]{:S(2)}, u32[]{:S(2)}) %all-to-all-start.1) | async-done | bytes 524320 | tf_op jit(solution)/shard_map/all_to_all | solution.py:416
  82.4 1.4 %gate_results.1 = (bf16[128,1024]{1,0:T(8,128)(2,1)}, bf16[128,1024]{1,0:T(8,128)(2,1)}, bf16[128,1024]{1,0:T(8,128)(2,1)}, bf16[128,1024]{1,0:T(8,128)(2,1)}) custom-call(bf16[128,1024]{1,0:T(8,128)(2,1)S(1)} %copy-done, bf16[128,1024]{1,0:T(8,128)(2,1)S(1)} %copy-done.1, bf16[128,1024]{1,0:T(8,128)(2,1)S(1)} %copy-done.2, bf16[128,1024]{1,0:T(8,128)(2,1)S(1)} %copy-done.3, ...), custom_call_target="tpu_custom_call" | custom-call | flops 2000000000 | bytes 1024 | tf_op jit(solution)/shard_map/gate_results/pallas_call | solution.py:365
  (15 shorter events, 0.0 us)
Async XLA Ops:
  0.6 19.0 %collective-permute-start = (bf16[16,8192]{1,0:T(8,128)(2,1)}, bf16[16,8192]{1,0:T(8,128)(2,1)S(1)}, u32[]{:S(2)}, u32[]{:S(2)}) collective-permute-start(bf16[16,8192]{1,0:T(8,128)(2,1)} %bitcast.6), channel_id=1, source_target_pairs={{0,0},{1,64},{2,128},{3,192},{4,4},{5,68},{6,132},{7,196},{8,8},{9... | collective-permute-start | bytes 786440 | tf_op jit(solution)/shard_map/ppermute | solution.py:409
  4.5 35.0 %all-to-all-start = ((bf16[64,2,16,128]{3,2,1,0:T(8,128)(2,1)}), bf16[64,2,16,128]{3,2,1,0:T(8,128)(2,1)S(1)}, u32[]{:S(2)}, u32[]{:S(2)}) async-start(bf16[64,2,16,128]{3,2,1,0:T(8,128)(2,1)} %bitcast.5), calls=%async_computation | async-start | bytes 1048576 | tf_op jit(solution)/shard_map/all_to_all | solution.py:413
  19.5 20.1 %copy-start.4 = (bf16[768,256]{1,0:T(8,128)(2,1)S(1)}, bf16[768,256]{1,0:T(8,128)(2,1)}, u32[]{:S(2)}) copy-start(bf16[768,256]{1,0:T(8,128)(2,1)} %constant.18.clone.second.second_far) | copy-start | bytes 1179652
  19.5 20.0 %copy-start.5 = (bf16[768,256]{1,0:T(8,128)(2,1)S(1)}, bf16[768,256]{1,0:T(8,128)(2,1)}, u32[]{:S(2)}) copy-start(bf16[768,256]{1,0:T(8,128)(2,1)} %constant.19.clone.second_back_far) | copy-start | bytes 1179652
  19.5 20.0 %copy-start.6 = (bf16[128,768]{1,0:T(8,128)(2,1)S(1)}, bf16[128,768]{1,0:T(8,128)(2,1)}, u32[]{:S(2)}) copy-start(bf16[128,768]{1,0:T(8,128)(2,1)} %constant.20.clone.first_back_far) | copy-start | bytes 589828
  19.5 20.0 %copy-start.7 = (bf16[256,256]{1,0:T(8,128)(2,1)S(1)}, bf16[256,256]{1,0:T(8,128)(2,1)}, u32[]{:S(2)}) copy-start(bf16[256,256]{1,0:T(8,128)(2,1)} %constant.16.clone.first_far) | copy-start | bytes 393220
  19.6 20.0 %copy-start.8 = (bf16[64,768]{1,0:T(8,128)(2,1)S(1)}, bf16[64,768]{1,0:T(8,128)(2,1)}, u32[]{:S(2)}) copy-start(bf16[64,768]{1,0:T(8,128)(2,1)} %constant.21.clone.first_back_imag_far) | copy-start | bytes 294916
  19.6 20.0 %copy-start.9 = (f32[128,128]{1,0:T(8,128)S(1)}, f32[128,128]{1,0:T(8,128)}, u32[]{:S(2)}) copy-start(f32[128,128]{1,0:T(8,128)} %constant.23.clone.turn_sin.turn_sin_far) | copy-start | bytes 196612
  19.6 20.0 %copy-start.10 = (f32[128,128]{1,0:T(8,128)S(1)}, f32[128,128]{1,0:T(8,128)}, u32[]{:S(2)}) copy-start(f32[128,128]{1,0:T(8,128)} %constant.22.clone.turn_cos.turn_cos_far) | copy-start | bytes 196612
  19.6 0.7 copy-start.12
  39.6 1.6 %copy-start.11 = (f32[16,128,256]{2,1,0:T(8,128)S(1)}, f32[16,128,256]{2,1,0:T(8,128)}, u32[]{:S(2)}) copy-start(f32[16,128,256]{2,1,0:T(8,128)} %filter_spectra.1.spectrum_far) | copy-start | bytes 6291460
  53.6 11.7 %collective-permute-start.1 = (bf16[64,16,128]{2,1,0:T(8,128)(2,1)S(1)}, bf16[64,16,128]{2,1,0:T(8,128)(2,1)S(1)}, u32[]{:S(2)}, u32[]{:S(2)}) collective-permute-start(bf16[64,16,128]{2,1,0:T(8,128)(2,1)S(1)} %get-tuple-element.16), channel_id=1, source_target_pairs={{0,0},{1,64},{2,128},{3,192},{4,4},{5,68},{6,132},{7,196},{8,8},{9... | collective-permute-start | bytes 786440 | tf_op jit(solution)/shard_map/ppermute | solution.py:415
  54.2 28.1 %all-to-all-start.1 = ((bf16[64,2,16,128]{3,2,1,0:T(8,128)(2,1)}), bf16[64,2,16,128]{3,2,1,0:T(8,128)(2,1)S(1)}, u32[]{:S(2)}, u32[]{:S(2)}) async-start(bf16[64,2,16,128]{3,2,1,0:T(8,128)(2,1)} %get-tuple-element.11), calls=%async_computation.1 | async-start | bytes 1048576 | tf_op jit(solution)/shard_map/all_to_all | solution.py:416
  65.2 17.2 %copy-start = (bf16[128,1024]{1,0:T(8,128)(2,1)S(1)}, bf16[128,1024]{1,0:T(8,128)(2,1)}, u32[]{:S(2)}) copy-start(bf16[128,1024]{1,0:T(8,128)(2,1)} %out_gate.3) | copy-start | bytes 786436
  65.2 17.2 %copy-start.1 = (bf16[128,1024]{1,0:T(8,128)(2,1)S(1)}, bf16[128,1024]{1,0:T(8,128)(2,1)}, u32[]{:S(2)}) copy-start(bf16[128,1024]{1,0:T(8,128)(2,1)} %in_gate.3) | copy-start | bytes 786436
  65.2 17.1 %copy-start.2 = (bf16[128,1024]{1,0:T(8,128)(2,1)S(1)}, bf16[128,1024]{1,0:T(8,128)(2,1)}, u32[]{:S(2)}) copy-start(bf16[128,1024]{1,0:T(8,128)(2,1)} %values.3) | copy-start | bytes 786436
  65.2 17.1 %copy-start.3 = (bf16[128,1024]{1,0:T(8,128)(2,1)S(1)}, bf16[128,1024]{1,0:T(8,128)(2,1)}, u32[]{:S(2)}) copy-start(bf16[128,1024]{1,0:T(8,128)(2,1)} %cotan.3) | copy-start | bytes 786436

commit v3 on v2

--- a/solution.py
+++ b/solution.py
@@ -10,7 +10,7 @@
 from jax.sharding import PartitionSpec as P
 
 LANES = 128
-TOGETHER = 2
+TOGETHER = 8
 WIDE = jnp.float32
 NARROW = jnp.bfloat16
 
@@ -337,7 +337,7 @@
             pltpu.SemaphoreType.DMA((len(operands),)),
             pltpu.SemaphoreType.DMA((4,)),
         ],
-        compiler_params=params(48),
+        compiler_params=params(50),
         cost_estimate=cost(6),
         name="convolutions",
     )(*operands)
@@ -369,7 +369,7 @@
         + [pl.BlockSpec((groups, per_group // steps, 2, owned, LANES), lambda i: (0, i, 0, 0, 0))],
         out_specs=[block] * 4,
         out_shape=[jax.ShapeDtypeStruct(out_gate.shape, NARROW)] * 4,
-        compiler_params=params(48),
+        compiler_params=params(50),
         cost_estimate=cost(2),
         name="gate_results",
     )(out_gate, in_gate, values, cotan, received)
@@ -388,7 +388,7 @@
     return pl.pallas_call(
         filter_kernel,
         out_shape=jax.ShapeDtypeStruct((owned, blocks * LANES), WIDE),
-        compiler_params=params(48),
+        compiler_params=params(50),
         cost_estimate=cost(12),
         name="filter_results",
     )(received)

time: 84.1 us -> 78.2 us (0.930)
  Pallas kernels: 22.8 us -> 16.9 us
  local copies, waits for them, and re-layouts: 2.35 us -> 0.77 us
  waiting for transfers between devices: 29.7 us -> 31.1 us
    pallas_call x1, Pallas kernels: 12.3 us -> 8 us  [convolutions(): pl.pallas_call(functools.partial(convolution_kernel, scale / (LANES * LAN...]
    unnamed x26 -> x24, local copies, waits for them, and re-layouts: 2.35 us -> 0.77 us
    all_to_all x1, waiting for transfers between devices: 13.6 us -> 15 us  [per_device(): lax.all_to_all(sections, 'seq', split_axis=0, concat_axis=0, tiled=True)]
    pallas_call x1, Pallas kernels: 5.69 us -> 4.23 us  [filter_spectra(): pl.pallas_call(spectrum_kernel, in_specs=in_vmem(5), out_specs=in_vmem(1)...]
  transfers between devices with their start and end apart: 4 -> 4, of which waited for: 2 -> 2; matrix products, arithmetic and copies ran while one was open for 0% -> 0% of each run, Pallas kernels for 11% -> 10%
where the time goes in v3:
time: 78.2 us; the launch traced here: 77.9 us
  waiting for transfers between devices  31.1 us (40%)
  starting transfers between devices  28.2 us (36%)
  Pallas kernels  16.9 us (22%)
  between operations  0.82 us (1%)
    all_to_all x1, waiting for transfers between devices, per_device(): lax.all_to_all(back, 'seq', split_axis=0, concat_axis=0, tiled=True)  16.1 us
    all_to_all x1, waiting for transfers between devices, per_device(): lax.all_to_all(sections, 'seq', split_axis=0, concat_axis=0, tiled=True)  15 us
    all_to_all x1, starting transfers between devices, per_device(): lax.all_to_all(sections, 'seq', split_axis=0, concat_axis=0, tiled=True)  15 us
    all_to_all x1, starting transfers between devices, per_device(): lax.all_to_all(back, 'seq', split_axis=0, concat_axis=0, tiled=True)  10.9 us
    pallas_call x1, Pallas kernels, convolutions(): pl.pallas_call(functools.partial(convolution_kernel, scale / (LANES * LAN...  8 us
    pallas_call x1, Pallas kernels, filter_spectra(): pl.pallas_call(spectrum_kernel, in_specs=in_vmem(5), out_specs=in_vmem(1)...  4.23 us
    pallas_call x1, Pallas kernels, gates(): pl.pallas_call(gate_kernel, grid=(steps,), in_specs=[block] * 4, out_spec...  2.27 us
    ppermute x1, starting transfers between devices, per_device(): filters_here = lax.ppermute(filters.T, ('seq', 'ch'), swap)  1.61 us
  transfers between devices with their start and end apart: 4, of which 2 were waited for; matrix products, arithmetic and copies ran while one was open for 0% of the time, Pallas kernels for 10%

profile of v3, /device:TPU:2, one launch (start us, length us, event | category | flops | bytes accessed | tf_op | source)
XLA Modules:
  0.0 77.9 jit_solution(4896733063788380444)
XLA Ops:
  0.6 1.6 %collective-permute-start = (bf16[16,8192]{1,0:T(8,128)(2,1)}, bf16[16,8192]{1,0:T(8,128)(2,1)S(1)}, u32[]{:S(2)}, u32[]{:S(2)}) collective-permute-start(bf16[16,8192]{1,0:T(8,128)(2,1)} %bitcast.6), channel_id=1, source_target_pairs={{0,0},{1,64},{2,128},{3,192},{4,4},{5,68},{6,132},{7,196},{8,8},{9... | collective-permute-start | bytes 786440 | tf_op jit(solution)/shard_map/ppermute | solution.py:409
  2.2 2.3 %gate_products.1 = bf16[4,16,2,16,128]{4,3,2,1,0:T(8,128)(2,1)} custom-call(bf16[128,1024]{1,0:T(8,128)(2,1)} %out_gate.3, bf16[128,1024]{1,0:T(8,128)(2,1)} %in_gate.3, bf16[128,1024]{1,0:T(8,128)(2,1)} %values.3, bf16[128,1024]{1,0:T(8,128)(2,1)} %cotan.3), custom_call_target="tpu_custom_call" | custom-call | flops 2000000000 | bytes 1024 | tf_op jit(solution)/shard_map/gate_products/pallas_call | solution.py:42
  4.5 15.0 %all-to-all-start = ((bf16[64,2,16,128]{3,2,1,0:T(8,128)(2,1)}), bf16[64,2,16,128]{3,2,1,0:T(8,128)(2,1)S(1)}, u32[]{:S(2)}, u32[]{:S(2)}) async-start(bf16[64,2,16,128]{3,2,1,0:T(8,128)(2,1)} %bitcast.5), calls=%async_computation | async-start | bytes 1048576 | tf_op jit(solution)/shard_map/all_to_all | solution.py:413
  19.5 0.0 copy-start.4
  19.5 0.0 copy-start.5
  19.5 0.0 copy-start.6
  19.5 0.0 copy-start.7
  19.6 0.0 copy-start.8
  19.6 0.0 copy-start.9
  19.6 0.0 copy-start.10
  19.6 0.0 copy-start.11
  19.6 0.7 copy-done.11
  20.3 4.2 %filter_spectra.1.spectrum_far = f32[16,128,256]{2,1,0:T(8,128)} custom-call(bf16[16,8192]{1,0:T(8,128)(2,1)} %copy-done.11, bf16[256,128]{1,0:T(8,128)(2,1)} %constant.17.clone.first, bf16[768,256]{1,0:T(8,128)(2,1)} %constant.18.clone.second.second_far, f32[128,128]{1,0:T(8,128)} %constant.22.clone.turn_cos.turn_cos_far, ...), custom_call_target="tpu_custom_call" | custom-call | flops 12000000000 | bytes 1024 | tf_op jit(solution)/shard_map/filter_spectra/pallas_call | solution.py:297
  24.5 15.0 %all-to-all-done.received_far = bf16[64,2,16,128]{3,2,1,0:T(8,128)(2,1)S(1)} async-done(((bf16[64,2,16,128]{3,2,1,0:T(8,128)(2,1)}), bf16[64,2,16,128]{3,2,1,0:T(8,128)(2,1)S(1)}, u32[]{:S(2)}, u32[]{:S(2)}) %all-to-all-start) | async-done | bytes 524320 | tf_op jit(solution)/shard_map/all_to_all | solution.py:413
  39.6 8.0 %convolutions.1 = (bf16[64,2,16,128]{3,2,1,0:T(8,128)(2,1)}, bf16[64,16,128]{2,1,0:T(8,128)(2,1)S(1)}) custom-call(bf16[64,2,16,128]{3,2,1,0:T(8,128)(2,1)S(1)} %all-to-all-done.received_far, f32[16,128,256]{2,1,0:T(8,128)} %filter_spectra.1.spectrum_far, bf16[256,256]{1,0:T(8,128)(2,1)S(1)} %copy-done.7, bf16[768,256]{1,0:T(8,128)(2,1)S(1)} %copy-done.4, ...), custom_call_target="tpu_custom_call" | custom-call | flops 6000000000 | bytes 1024 | tf_op jit(solution)/shard_map/convolutions/pallas_call | solution.py:323
  47.6 0.7 collective-permute-start.1
  48.3 10.9 %all-to-all-start.1 = ((bf16[64,2,16,128]{3,2,1,0:T(8,128)(2,1)}), bf16[64,2,16,128]{3,2,1,0:T(8,128)(2,1)S(1)}, u32[]{:S(2)}, u32[]{:S(2)}) async-start(bf16[64,2,16,128]{3,2,1,0:T(8,128)(2,1)} %get-tuple-element.11), calls=%async_computation.1 | async-start | bytes 1048576 | tf_op jit(solution)/shard_map/all_to_all | solution.py:416
  59.2 0.0 copy-start
  59.2 0.0 copy-start.1
  59.3 0.0 copy-start.2
  59.3 0.0 copy-start.3
  59.3 1.0 %filter_results.1 = f32[16,8192]{1,0:T(8,128)} custom-call(bf16[64,16,128]{2,1,0:T(8,128)(2,1)S(1)} %collective-permute-done.1.received), custom_call_target="tpu_custom_call" | custom-call | flops 12000000000 | bytes 1024 | tf_op jit(solution)/shard_map/filter_results/pallas_call | solution.py:388
  60.3 16.1 %all-to-all-done.1 = bf16[64,2,16,128]{3,2,1,0:T(8,128)(2,1)S(1)} async-done(((bf16[64,2,16,128]{3,2,1,0:T(8,128)(2,1)}), bf16[64,2,16,128]{3,2,1,0:T(8,128)(2,1)S(1)}, u32[]{:S(2)}, u32[]{:S(2)}) %all-to-all-start.1) | async-done | bytes 524320 | tf_op jit(solution)/shard_map/all_to_all | solution.py:416
  76.4 1.4 %gate_results.1 = (bf16[128,1024]{1,0:T(8,128)(2,1)}, bf16[128,1024]{1,0:T(8,128)(2,1)}, bf16[128,1024]{1,0:T(8,128)(2,1)}, bf16[128,1024]{1,0:T(8,128)(2,1)}) custom-call(bf16[128,1024]{1,0:T(8,128)(2,1)S(1)} %copy-done, bf16[128,1024]{1,0:T(8,128)(2,1)S(1)} %copy-done.1, bf16[128,1024]{1,0:T(8,128)(2,1)S(1)} %copy-done.2, bf16[128,1024]{1,0:T(8,128)(2,1)S(1)} %copy-done.3, ...), custom_call_target="tpu_custom_call" | custom-call | flops 2000000000 | bytes 1024 | tf_op jit(solution)/shard_map/gate_results/pallas_call | solution.py:365
  (13 shorter events, 0.0 us)
Async XLA Ops:
  0.6 19.0 %collective-permute-start = (bf16[16,8192]{1,0:T(8,128)(2,1)}, bf16[16,8192]{1,0:T(8,128)(2,1)S(1)}, u32[]{:S(2)}, u32[]{:S(2)}) collective-permute-start(bf16[16,8192]{1,0:T(8,128)(2,1)} %bitcast.6), channel_id=1, source_target_pairs={{0,0},{1,64},{2,128},{3,192},{4,4},{5,68},{6,132},{7,196},{8,8},{9... | collective-permute-start | bytes 786440 | tf_op jit(solution)/shard_map/ppermute | solution.py:409
  4.5 35.0 %all-to-all-start = ((bf16[64,2,16,128]{3,2,1,0:T(8,128)(2,1)}), bf16[64,2,16,128]{3,2,1,0:T(8,128)(2,1)S(1)}, u32[]{:S(2)}, u32[]{:S(2)}) async-start(bf16[64,2,16,128]{3,2,1,0:T(8,128)(2,1)} %bitcast.5), calls=%async_computation | async-start | bytes 1048576 | tf_op jit(solution)/shard_map/all_to_all | solution.py:413
  19.5 20.1 %copy-start.4 = (bf16[768,256]{1,0:T(8,128)(2,1)S(1)}, bf16[768,256]{1,0:T(8,128)(2,1)}, u32[]{:S(2)}) copy-start(bf16[768,256]{1,0:T(8,128)(2,1)} %constant.18.clone.second.second_far) | copy-start | bytes 1179652
  19.5 20.0 %copy-start.5 = (bf16[768,256]{1,0:T(8,128)(2,1)S(1)}, bf16[768,256]{1,0:T(8,128)(2,1)}, u32[]{:S(2)}) copy-start(bf16[768,256]{1,0:T(8,128)(2,1)} %constant.19.clone.second_back_far) | copy-start | bytes 1179652
  19.5 20.0 %copy-start.6 = (bf16[128,768]{1,0:T(8,128)(2,1)S(1)}, bf16[128,768]{1,0:T(8,128)(2,1)}, u32[]{:S(2)}) copy-start(bf16[128,768]{1,0:T(8,128)(2,1)} %constant.20.clone.first_back_far) | copy-start | bytes 589828
  19.5 20.0 %copy-start.7 = (bf16[256,256]{1,0:T(8,128)(2,1)S(1)}, bf16[256,256]{1,0:T(8,128)(2,1)}, u32[]{:S(2)}) copy-start(bf16[256,256]{1,0:T(8,128)(2,1)} %constant.16.clone.first_far) | copy-start | bytes 393220
  19.6 20.0 %copy-start.8 = (bf16[64,768]{1,0:T(8,128)(2,1)S(1)}, bf16[64,768]{1,0:T(8,128)(2,1)}, u32[]{:S(2)}) copy-start(bf16[64,768]{1,0:T(8,128)(2,1)} %constant.21.clone.first_back_imag_far) | copy-start | bytes 294916
  19.6 20.0 %copy-start.9 = (f32[128,128]{1,0:T(8,128)S(1)}, f32[128,128]{1,0:T(8,128)}, u32[]{:S(2)}) copy-start(f32[128,128]{1,0:T(8,128)} %constant.23.clone.turn_sin.turn_sin_far) | copy-start | bytes 196612
  19.6 20.0 %copy-start.10 = (f32[128,128]{1,0:T(8,128)S(1)}, f32[128,128]{1,0:T(8,128)}, u32[]{:S(2)}) copy-start(f32[128,128]{1,0:T(8,128)} %constant.22.clone.turn_cos.turn_cos_far) | copy-start | bytes 196612
  19.6 0.7 copy-start.11
  47.6 11.7 %collective-permute-start.1 = (bf16[64,16,128]{2,1,0:T(8,128)(2,1)S(1)}, bf16[64,16,128]{2,1,0:T(8,128)(2,1)S(1)}, u32[]{:S(2)}, u32[]{:S(2)}) collective-permute-start(bf16[64,16,128]{2,1,0:T(8,128)(2,1)S(1)} %get-tuple-element.16), channel_id=1, source_target_pairs={{0,0},{1,64},{2,128},{3,192},{4,4},{5,68},{6,132},{7,196},{8,8},{9... | collective-permute-start | bytes 786440 | tf_op jit(solution)/shard_map/ppermute | solution.py:415
  48.3 28.1 %all-to-all-start.1 = ((bf16[64,2,16,128]{3,2,1,0:T(8,128)(2,1)}), bf16[64,2,16,128]{3,2,1,0:T(8,128)(2,1)S(1)}, u32[]{:S(2)}, u32[]{:S(2)}) async-start(bf16[64,2,16,128]{3,2,1,0:T(8,128)(2,1)} %get-tuple-element.11), calls=%async_computation.1 | async-start | bytes 1048576 | tf_op jit(solution)/shard_map/all_to_all | solution.py:416
  59.2 17.2 %copy-start = (bf16[128,1024]{1,0:T(8,128)(2,1)S(1)}, bf16[128,1024]{1,0:T(8,128)(2,1)}, u32[]{:S(2)}) copy-start(bf16[128,1024]{1,0:T(8,128)(2,1)} %out_gate.3) | copy-start | bytes 786436
  59.2 17.2 %copy-start.1 = (bf16[128,1024]{1,0:T(8,128)(2,1)S(1)}, bf16[128,1024]{1,0:T(8,128)(2,1)}, u32[]{:S(2)}) copy-start(bf16[128,1024]{1,0:T(8,128)(2,1)} %in_gate.3) | copy-start | bytes 786436
  59.3 17.2 %copy-start.2 = (bf16[128,1024]{1,0:T(8,128)(2,1)S(1)}, bf16[128,1024]{1,0:T(8,128)(2,1)}, u32[]{:S(2)}) copy-start(bf16[128,1024]{1,0:T(8,128)(2,1)} %values.3) | copy-start | bytes 786436
  59.3 17.2 %copy-start.3 = (bf16[128,1024]{1,0:T(8,128)(2,1)S(1)}, bf16[128,1024]{1,0:T(8,128)(2,1)}, u32[]{:S(2)}) copy-start(bf16[128,1024]{1,0:T(8,128)(2,1)} %cotan.3) | copy-start | bytes 786436

commit v4 on v3

--- a/solution.py
+++ b/solution.py
@@ -11,6 +11,7 @@
 
 LANES = 128
 TOGETHER = 8
+GROUP = 4
 WIDE = jnp.float32
 NARROW = jnp.bfloat16
 
@@ -83,10 +84,10 @@
         "first_real": across(np.block([[near_cos], [-near_sin]]), (0, 1)),
         "second": down(np.block([[cos, -sin], [sin, cos]]), (0, 0, 1)),
         "second_back": down(np.block([[cos, sin], [-sin, cos]]), (0, 0, 1)),
-        "first_back": across(
-            np.block([[near_cos.T, -near_sin.T], [near_sin.T, near_cos.T]]), (0, 0, 1)
+        "first_back": down(
+            np.block([[near_cos.T, -near_sin.T], [near_sin.T, near_cos.T]]), (0, 1)
         ),
-        "first_back_imag": across(np.block([[near_sin.T, near_cos.T]]), (0, 0, 1)),
+        "first_back_imag": down(np.block([[near_sin.T, near_cos.T]]), (0, 1)),
         "turn_cos": np.cos(turn).astype(np.float32),
         "turn_sin": np.sin(turn).astype(np.float32),
     }
@@ -96,38 +97,61 @@
     return jnp.dot(left, right, preferred_element_type=WIDE)
 
 
-def three_parts(real, imag, axis):
+def three_parts(real, imag):
     real_high, real_low = split(real)
     imag_high, imag_low = split(imag)
-    return jnp.concatenate(
-        [real_high, imag_high, real_low, imag_low, real_high, imag_high], axis=axis
-    )
+    return jnp.concatenate([real_high, imag_high, real_low, imag_low, real_high, imag_high], axis=1)
+
+
+def grouped_dot(left, right):
+    out = []
+    for at in range(0, len(left), GROUP):
+        group = left[at : at + GROUP]
+        found = dot(jnp.concatenate(group, axis=0), right[...])
+        out += [found[one * LANES : (one + 1) * LANES] for one in range(len(group))]
+    return out
 
 
 def spectra(data, first, second, turn_cos, turn_sin):
     stacked = jnp.concatenate([jnp.concatenate([one, one], axis=0) for one in data], axis=1)
     sections = dot(first[...], stacked)
-    out = []
+    turned = []
     for at in range(len(data)):
         real = sections[:LANES, at * LANES : (at + 1) * LANES]
         imag = sections[LANES:, at * LANES : (at + 1) * LANES]
         turned_real = real * turn_cos[...] + imag * turn_sin[...]
         turned_imag = imag * turn_cos[...] - real * turn_sin[...]
-        spectrum = dot(three_parts(turned_real, turned_imag, 1), second[...])
-        out.append(spectrum)
+        turned.append(three_parts(turned_real, turned_imag))
+    found = grouped_dot(turned, second)
+    return [found[at] for at in range(len(data))]
+
+
+def sections_back(spectrum, second_back, turn_cos, turn_sin):
+    parts = grouped_dot([three_parts(real, imag) for real, imag in spectrum], second_back)
+    turned = []
+    for at in range(len(spectrum)):
+        real, imag = parts[at][:, :LANES], parts[at][:, LANES:]
+        real_high, real_low = split(real * turn_cos[...] - imag * turn_sin[...])
+        imag_high, imag_low = split(imag * turn_cos[...] + real * turn_sin[...])
+        turned.append(
+            (
+                jnp.concatenate([real_high, imag_high], axis=0),
+                jnp.concatenate([real_low, imag_low], axis=0),
+            )
+        )
+    return turned
+
+
+def signals(turned, first_back):
+    rows = first_back.shape[0] // 2
+    out = []
+    for at in range(0, len(turned), 2):
+        high = jnp.concatenate([one[0] for one in turned[at : at + 2]], axis=1)
+        low = jnp.concatenate([one[1] for one in turned[at : at + 2]], axis=1)
+        both = dot(first_back[...], high)
+        result = both[:rows] + both[rows:] + dot(first_back[pl.ds(0, rows), :], low)
+        out += [result[:, :LANES], result[:, LANES:]]
     return out
-
-
-def signals(spectrum, first_back, second_back, turn_cos, turn_sin):
-    turned = []
-    for real, imag in spectrum:
-        part = dot(three_parts(real, imag, 1), second_back[...])
-        real, imag = part[:, :LANES], part[:, LANES:]
-        turned_real = real * turn_cos[...] - imag * turn_sin[...]
-        turned_imag = imag * turn_cos[...] + real * turn_sin[...]
-        turned.append(three_parts(turned_real, turned_imag, 0))
-    result = dot(first_back[...], jnp.concatenate(turned, axis=1))
-    return [result[:, at * LANES : (at + 1) * LANES] for at in range(len(spectrum))]
 
 
 def spectrum_kernel(filters, first, second, turn_cos, turn_sin, spectrum, taps):
@@ -158,19 +182,8 @@
 
 def convolution_kernel(
     scale,
-    received_far,
+    received,
     spectrum_far,
-    first_far,
-    second_far,
-    first_back_far,
-    second_back_far,
-    turn_cos_far,
-    turn_sin_far,
-    first_back_imag_far,
-    send_far,
-    grad_filters,
-    received,
-    filter_spectrum,
     first,
     second,
     first_back,
@@ -178,6 +191,9 @@
     turn_cos,
     turn_sin,
     first_back_imag,
+    send_far,
+    grad_filters,
+    filter_spectrum,
     send,
     signal,
     back,
@@ -186,35 +202,8 @@
     sent,
 ):
     blocks, _, owned, _ = received.shape
-    far = (
-        received_far,
-        first_far,
-        turn_cos_far,
-        turn_sin_far,
-        second_far,
-        spectrum_far,
-        second_back_far,
-        first_back_far,
-        first_back_imag_far,
-    )
-    near = (
-        received,
-        first,
-        turn_cos,
-        turn_sin,
-        second,
-        filter_spectrum,
-        second_back,
-        first_back,
-        first_back_imag,
-    )
-    loads = [
-        pltpu.make_async_copy(one, other, loaded.at[at])
-        for at, (one, other) in enumerate(zip(far, near))
-    ]
-    for load in loads:
-        load.start()
-    loads[0].wait()
+    load = pltpu.make_async_copy(spectrum_far, filter_spectrum, loaded)
+    load.start()
     ups = []
     for which in range(2):
         size = jnp.zeros((owned, LANES), WIDE)
@@ -226,8 +215,7 @@
         for j in range(blocks):
             at = j if which == 0 else blocks - 1 - j
             signal[which, pl.ds(at * owned, owned), :] = received[j, which].astype(WIDE) * down
-    for load in loads[1:]:
-        load.wait()
+    load.wait()
 
     def pair(at, carry):
         data = []
@@ -248,13 +236,14 @@
             products.append(
                 (real * taps_real - imag * taps_imag, real * taps_imag + imag * taps_real)
             )
-        result = signals(products, first_back, second_back, turn_cos, turn_sin)
+        turned = sections_back(products + squares, second_back, turn_cos, turn_sin)
+        result = signals(turned[:TOGETHER], first_back)
         for c in range(TOGETHER):
             for which in range(2):
                 back[which, pl.ds(TOGETHER * at + c, blocks, stride=owned), :] = result[c][
                     which * blocks : (which + 1) * blocks
                 ]
-        result = signals(squares, first_back_imag, second_back, turn_cos, turn_sin)
+        result = signals(turned[TOGETHER:], first_back_imag)
         for c in range(TOGETHER):
             grads[pl.ds(TOGETHER * at + c, blocks, stride=owned), :] = result[c]
         return carry
@@ -322,19 +311,19 @@
     far = pl.BlockSpec(memory_space=pl.ANY)
     return pl.pallas_call(
         functools.partial(convolution_kernel, scale / (LANES * LANES)),
-        in_specs=[far] * len(operands),
+        in_specs=in_vmem(1) + [far] + in_vmem(7),
         out_specs=[far] + in_vmem(1),
         out_shape=[
             jax.ShapeDtypeStruct(received.shape, NARROW),
             jax.ShapeDtypeStruct((blocks, owned, LANES), NARROW),
         ],
-        scratch_shapes=[pltpu.VMEM(one.shape, one.dtype) for one in operands]
-        + [
+        scratch_shapes=[
+            pltpu.VMEM(filter_spectrum.shape, WIDE),
             pltpu.VMEM(received.shape, NARROW),
             pltpu.VMEM((2, blocks * owned, LANES), WIDE),
             pltpu.VMEM((2, blocks * owned, LANES), WIDE),
             pltpu.VMEM((blocks * owned, LANES), WIDE),
-            pltpu.SemaphoreType.DMA((len(operands),)),
+            pltpu.SemaphoreType.DMA,
             pltpu.SemaphoreType.DMA((4,)),
         ],
         compiler_params=params(50),
@@ -406,9 +395,10 @@
             high, low = divmod(s, per_group)
             swap.append((s * chan_count + c, (c * per_group + low) * chan_count + high))
     tables = {name: jnp.asarray(table) for name, table in dft_tables(seq_count).items()}
-    filters_here = lax.ppermute(filters.T, ("seq", "ch"), swap)
+    send = gates(output_gate, input_gate, values_in, cotangent, seq_count, chan_count)
+    filters_owned, send = lax.optimization_barrier((filters.T, send))
+    filters_here = lax.ppermute(filters_owned, ("seq", "ch"), swap)
     filter_spectrum = filter_spectra(filters_here, tables)
-    send = gates(output_gate, input_gate, values_in, cotangent, seq_count, chan_count)
     sections = send.reshape(seq_count, 2, owned, LANES)
     received = lax.all_to_all(sections, "seq", split_axis=0, concat_axis=0, tiled=True)
     back, grads = convolutions(received, filter_spectrum, tables, scale)

time: 78.2 us -> 77.2 us (0.987)
  Pallas kernels: 16.9 us -> 15.8 us
    pallas_call x1, Pallas kernels: 8 us -> 6.92 us  [convolutions(): pl.pallas_call(functools.partial(convolution_kernel, scale / (LANES * LAN...]
    ppermute x1, starting transfers between devices: 1.61 us -> 0.67 us  [per_device(): filters_here = lax.ppermute(filters_owned, ('seq', 'ch'), swap)]
    all_to_all x1, starting transfers between devices: 15 us -> 15.9 us  [per_device(): lax.all_to_all(sections, 'seq', split_axis=0, concat_axis=0, tiled=True)]
  transfers between devices with their start and end apart: 4 -> 4, of which waited for: 2 -> 2; matrix products, arithmetic and copies ran while one was open for 0% -> 0% of each run, Pallas kernels for 10% -> 7%
where the time goes in v4:
time: 77.2 us; the launch traced here: 76.8 us
  waiting for transfers between devices  31.2 us (40%)
  starting transfers between devices  28.2 us (37%)
  Pallas kernels  15.8 us (20%)
  between operations  0.84 us (1%)
    all_to_all x1, waiting for transfers between devices, per_device(): lax.all_to_all(back, 'seq', split_axis=0, concat_axis=0, tiled=True)  16.1 us
    all_to_all x1, starting transfers between devices, per_device(): lax.all_to_all(sections, 'seq', split_axis=0, concat_axis=0, tiled=True)  15.9 us
    all_to_all x1, waiting for transfers between devices, per_device(): lax.all_to_all(sections, 'seq', split_axis=0, concat_axis=0, tiled=True)  15.1 us
    all_to_all x1, starting transfers between devices, per_device(): lax.all_to_all(back, 'seq', split_axis=0, concat_axis=0, tiled=True)  10.9 us
    pallas_call x1, Pallas kernels, convolutions(): pl.pallas_call(functools.partial(convolution_kernel, scale / (LANES * LAN...  6.92 us
    pallas_call x1, Pallas kernels, filter_spectra(): pl.pallas_call(spectrum_kernel, in_specs=in_vmem(5), out_specs=in_vmem(1)...  4.13 us
    pallas_call x1, Pallas kernels, gates(): pl.pallas_call(gate_kernel, grid=(steps,), in_specs=[block] * 4, out_spec...  2.33 us
  transfers between devices with their start and end apart: 4, of which 2 were waited for; matrix products, arithmetic and copies ran while one was open for 0% of the time, Pallas kernels for 7%

profile of v4, /device:TPU:2, one launch (start us, length us, event | category | flops | bytes accessed | tf_op | source)
XLA Modules:
  0.0 76.8 jit_solution(9786369606632222004)
XLA Ops:
  0.6 2.3 %gate_products.1 = bf16[4,16,2,16,128]{4,3,2,1,0:T(8,128)(2,1)} custom-call(bf16[128,1024]{1,0:T(8,128)(2,1)} %out_gate.3, bf16[128,1024]{1,0:T(8,128)(2,1)} %in_gate.3, bf16[128,1024]{1,0:T(8,128)(2,1)} %values.3, bf16[128,1024]{1,0:T(8,128)(2,1)} %cotan.3), custom_call_target="tpu_custom_call" | custom-call | flops 2000000000 | bytes 1024 | tf_op jit(solution)/shard_map/gate_products/pallas_call | solution.py:43
  3.0 0.7 collective-permute-start
  3.6 15.9 %all-to-all-start = ((bf16[64,2,16,128]{3,2,1,0:T(8,128)(2,1)}), bf16[64,2,16,128]{3,2,1,0:T(8,128)(2,1)S(1)}, u32[]{:S(2)}, u32[]{:S(2)}) async-start(bf16[64,2,16,128]{3,2,1,0:T(8,128)(2,1)} %bitcast.5), calls=%async_computation | async-start | bytes 1048576 | tf_op jit(solution)/shard_map/all_to_all | solution.py:403
  19.6 0.0 copy-start.4
  19.6 0.0 copy-start.5
  19.6 0.0 copy-start.6
  19.6 0.0 copy-start.7
  19.6 0.0 copy-start.8
  19.6 0.0 copy-start.9
  19.6 0.0 copy-start.10
  19.7 0.0 copy-start.12
  19.7 0.7 copy-done.12
  20.4 4.1 %filter_spectra.1.spectrum_far = f32[16,128,256]{2,1,0:T(8,128)} custom-call(bf16[16,8192]{1,0:T(8,128)(2,1)} %copy-done.12, bf16[256,128]{1,0:T(8,128)(2,1)} %constant.17.clone.first, bf16[768,256]{1,0:T(8,128)(2,1)} %constant.18.clone.second, f32[128,128]{1,0:T(8,128)} %constant.22.clone.turn_cos, f32[128,128]{1,0:T(8,128)} %constant.23.clone.turn_sin), custom_call_target="tpu_custom_call" | custom-call | flops 12000000000 | bytes 1024 | tf_op jit(solution)/shard_map/filter_spectra/pallas_call | solution.py:286
  24.5 15.1 %all-to-all-done.received = bf16[64,2,16,128]{3,2,1,0:T(8,128)(2,1)S(1)} async-done(((bf16[64,2,16,128]{3,2,1,0:T(8,128)(2,1)}), bf16[64,2,16,128]{3,2,1,0:T(8,128)(2,1)S(1)}, u32[]{:S(2)}, u32[]{:S(2)}) %all-to-all-start) | async-done | bytes 524320 | tf_op jit(solution)/shard_map/all_to_all | solution.py:403
  39.7 6.9 %convolutions.1 = (bf16[64,2,16,128]{3,2,1,0:T(8,128)(2,1)}, bf16[64,16,128]{2,1,0:T(8,128)(2,1)S(1)}) custom-call(bf16[64,2,16,128]{3,2,1,0:T(8,128)(2,1)S(1)} %all-to-all-done.received, f32[16,128,256]{2,1,0:T(8,128)} %filter_spectra.1.spectrum_far, bf16[256,256]{1,0:T(8,128)(2,1)S(1)} %copy-done.7, bf16[768,256]{1,0:T(8,128)(2,1)S(1)} %copy-done.4, ...), custom_call_target="tpu_custom_call" | custom-call | flops 6000000000 | bytes 1024 | tf_op jit(solution)/shard_map/convolutions/pallas_call | solution.py:312
  46.6 0.7 collective-permute-start.1
  47.3 10.9 %all-to-all-start.1 = ((bf16[64,2,16,128]{3,2,1,0:T(8,128)(2,1)}), bf16[64,2,16,128]{3,2,1,0:T(8,128)(2,1)S(1)}, u32[]{:S(2)}, u32[]{:S(2)}) async-start(bf16[64,2,16,128]{3,2,1,0:T(8,128)(2,1)} %get-tuple-element.15), calls=%async_computation.1 | async-start | bytes 1048576 | tf_op jit(solution)/shard_map/all_to_all | solution.py:406
  58.2 0.0 copy-start
  58.2 0.0 copy-start.1
  58.2 0.0 copy-start.2
  58.2 0.0 copy-start.3
  58.3 1.0 %filter_results.1 = f32[16,8192]{1,0:T(8,128)} custom-call(bf16[64,16,128]{2,1,0:T(8,128)(2,1)S(1)} %collective-permute-done.1.received), custom_call_target="tpu_custom_call" | custom-call | flops 12000000000 | bytes 1024 | tf_op jit(solution)/shard_map/filter_results/pallas_call | solution.py:377
  59.3 16.1 %all-to-all-done.1 = bf16[64,2,16,128]{3,2,1,0:T(8,128)(2,1)S(1)} async-done(((bf16[64,2,16,128]{3,2,1,0:T(8,128)(2,1)}), bf16[64,2,16,128]{3,2,1,0:T(8,128)(2,1)S(1)}, u32[]{:S(2)}, u32[]{:S(2)}) %all-to-all-start.1) | async-done | bytes 524320 | tf_op jit(solution)/shard_map/all_to_all | solution.py:406
  75.4 1.4 %gate_results.1 = (bf16[128,1024]{1,0:T(8,128)(2,1)}, bf16[128,1024]{1,0:T(8,128)(2,1)}, bf16[128,1024]{1,0:T(8,128)(2,1)}, bf16[128,1024]{1,0:T(8,128)(2,1)}) custom-call(bf16[128,1024]{1,0:T(8,128)(2,1)S(1)} %copy-done, bf16[128,1024]{1,0:T(8,128)(2,1)S(1)} %copy-done.1, bf16[128,1024]{1,0:T(8,128)(2,1)S(1)} %copy-done.2, bf16[128,1024]{1,0:T(8,128)(2,1)S(1)} %copy-done.3, ...), custom_call_target="tpu_custom_call" | custom-call | flops 2000000000 | bytes 1024 | tf_op jit(solution)/shard_map/gate_results/pallas_call | solution.py:354
  (15 shorter events, 0.0 us)
Async XLA Ops:
  0.6 2.3 %copy-start.11 = (bf16[8192,16]{0,1:T(8,128)(2,1)S(1)}, bf16[8192,16]{0,1:T(8,128)(2,1)}, u32[]{:S(2)}) copy-start(bf16[8192,16]{0,1:T(8,128)(2,1)} %param.16) | copy-start | bytes 786436
  3.0 16.7 %collective-permute-start = (bf16[16,8192]{1,0:T(8,128)(2,1)S(1)}, bf16[16,8192]{1,0:T(8,128)(2,1)S(1)}, u32[]{:S(2)}, u32[]{:S(2)}) collective-permute-start(bf16[16,8192]{1,0:T(8,128)(2,1)S(1)} %bitcast.6), channel_id=1, source_target_pairs={{0,0},{1,64},{2,128},{3,192},{4,4},{5,68},{6,132},{7,196},{8,8},{9... | collective-permute-start | bytes 786440 | tf_op jit(solution)/shard_map/ppermute | solution.py:400
  3.6 36.0 %all-to-all-start = ((bf16[64,2,16,128]{3,2,1,0:T(8,128)(2,1)}), bf16[64,2,16,128]{3,2,1,0:T(8,128)(2,1)S(1)}, u32[]{:S(2)}, u32[]{:S(2)}) async-start(bf16[64,2,16,128]{3,2,1,0:T(8,128)(2,1)} %bitcast.5), calls=%async_computation | async-start | bytes 1048576 | tf_op jit(solution)/shard_map/all_to_all | solution.py:403
  19.6 20.1 %copy-start.4 = (bf16[768,256]{1,0:T(8,128)(2,1)S(1)}, bf16[768,256]{1,0:T(8,128)(2,1)}, u32[]{:S(2)}) copy-start(bf16[768,256]{1,0:T(8,128)(2,1)} %constant.18.clone.second) | copy-start | bytes 1179652
  19.6 20.0 %copy-start.5 = (bf16[768,256]{1,0:T(8,128)(2,1)S(1)}, bf16[768,256]{1,0:T(8,128)(2,1)}, u32[]{:S(2)}) copy-start(bf16[768,256]{1,0:T(8,128)(2,1)} %constant.19.clone.second_back) | copy-start | bytes 1179652
  19.6 20.0 %copy-start.6 = (bf16[256,256]{1,0:T(8,128)(2,1)S(1)}, bf16[256,256]{1,0:T(8,128)(2,1)}, u32[]{:S(2)}) copy-start(bf16[256,256]{1,0:T(8,128)(2,1)} %constant.20.clone.first_back) | copy-start | bytes 393220
  19.6 20.0 %copy-start.7 = (bf16[256,256]{1,0:T(8,128)(2,1)S(1)}, bf16[256,256]{1,0:T(8,128)(2,1)}, u32[]{:S(2)}) copy-start(bf16[256,256]{1,0:T(8,128)(2,1)} %constant.16.clone.first) | copy-start | bytes 393220
  19.6 20.0 %copy-start.8 = (f32[128,128]{1,0:T(8,128)S(1)}, f32[128,128]{1,0:T(8,128)}, u32[]{:S(2)}) copy-start(f32[128,128]{1,0:T(8,128)} %constant.23.clone.turn_sin) | copy-start | bytes 196612
  19.6 20.0 %copy-start.9 = (f32[128,128]{1,0:T(8,128)S(1)}, f32[128,128]{1,0:T(8,128)}, u32[]{:S(2)}) copy-start(f32[128,128]{1,0:T(8,128)} %constant.22.clone.turn_cos) | copy-start | bytes 196612
  19.6 20.0 %copy-start.10 = (bf16[128,256]{1,0:T(8,128)(2,1)S(1)}, bf16[128,256]{1,0:T(8,128)(2,1)}, u32[]{:S(2)}) copy-start(bf16[128,256]{1,0:T(8,128)(2,1)} %constant.21.clone.first_back_imag) | copy-start | bytes 196612
  19.7 0.7 copy-start.12
  46.6 11.7 %collective-permute-start.1 = (bf16[64,16,128]{2,1,0:T(8,128)(2,1)S(1)}, bf16[64,16,128]{2,1,0:T(8,128)(2,1)S(1)}, u32[]{:S(2)}, u32[]{:S(2)}) collective-permute-start(bf16[64,16,128]{2,1,0:T(8,128)(2,1)S(1)} %get-tuple-element.20), channel_id=1, source_target_pairs={{0,0},{1,64},{2,128},{3,192},{4,4},{5,68},{6,132},{7,196},{8,8},{9... | collective-permute-start | bytes 786440 | tf_op jit(solution)/shard_map/ppermute | solution.py:405
  47.3 28.1 %all-to-all-start.1 = ((bf16[64,2,16,128]{3,2,1,0:T(8,128)(2,1)}), bf16[64,2,16,128]{3,2,1,0:T(8,128)(2,1)S(1)}, u32[]{:S(2)}, u32[]{:S(2)}) async-start(bf16[64,2,16,128]{3,2,1,0:T(8,128)(2,1)} %get-tuple-element.15), calls=%async_computation.1 | async-start | bytes 1048576 | tf_op jit(solution)/shard_map/all_to_all | solution.py:406
  58.2 17.2 %copy-start = (bf16[128,1024]{1,0:T(8,128)(2,1)S(1)}, bf16[128,1024]{1,0:T(8,128)(2,1)}, u32[]{:S(2)}) copy-start(bf16[128,1024]{1,0:T(8,128)(2,1)} %out_gate.3) | copy-start | bytes 786436
  58.2 17.2 %copy-start.1 = (bf16[128,1024]{1,0:T(8,128)(2,1)S(1)}, bf16[128,1024]{1,0:T(8,128)(2,1)}, u32[]{:S(2)}) copy-start(bf16[128,1024]{1,0:T(8,128)(2,1)} %in_gate.3) | copy-start | bytes 786436
  58.2 17.1 %copy-start.2 = (bf16[128,1024]{1,0:T(8,128)(2,1)S(1)}, bf16[128,1024]{1,0:T(8,128)(2,1)}, u32[]{:S(2)}) copy-start(bf16[128,1024]{1,0:T(8,128)(2,1)} %values.3) | copy-start | bytes 786436
  58.2 17.1 %copy-start.3 = (bf16[128,1024]{1,0:T(8,128)(2,1)S(1)}, bf16[128,1024]{1,0:T(8,128)(2,1)}, u32[]{:S(2)}) copy-start(bf16[128,1024]{1,0:T(8,128)(2,1)} %cotan.3) | copy-start | bytes 786436

commit v5 on v4

--- a/solution.py
+++ b/solution.py
@@ -202,8 +202,13 @@
     sent,
 ):
     blocks, _, owned, _ = received.shape
-    load = pltpu.make_async_copy(spectrum_far, filter_spectrum, loaded)
-    load.start()
+
+    def load(at):
+        rows = pl.ds(TOGETHER * at, TOGETHER)
+        return pltpu.make_async_copy(spectrum_far.at[rows], filter_spectrum.at[rows], loaded.at[at])
+
+    for at in range(owned // TOGETHER):
+        load(at).start()
     ups = []
     for which in range(2):
         size = jnp.zeros((owned, LANES), WIDE)
@@ -215,9 +220,9 @@
         for j in range(blocks):
             at = j if which == 0 else blocks - 1 - j
             signal[which, pl.ds(at * owned, owned), :] = received[j, which].astype(WIDE) * down
-    load.wait()
 
     def pair(at, carry):
+        load(at).wait()
         data = []
         for c in range(TOGETHER):
             rows = [
@@ -323,7 +328,7 @@
             pltpu.VMEM((2, blocks * owned, LANES), WIDE),
             pltpu.VMEM((2, blocks * owned, LANES), WIDE),
             pltpu.VMEM((blocks * owned, LANES), WIDE),
-            pltpu.SemaphoreType.DMA,
+            pltpu.SemaphoreType.DMA((owned // TOGETHER,)),
             pltpu.SemaphoreType.DMA((4,)),
         ],
         compiler_params=params(50),
@@ -405,10 +410,11 @@
     grads_owned = lax.ppermute(grads, ("seq", "ch"), swap)
     returned = lax.all_to_all(back, "seq", split_axis=0, concat_axis=0, tiled=True)
     returned = returned.reshape(chan_count, per_group, 2, owned, LANES)
-    grad_filters = filter_results(grads_owned).T
     output, grad_out, grad_in, grad_values = results(
         output_gate, input_gate, values_in, cotangent, returned
     )
+    grads_owned, output = lax.optimization_barrier((grads_owned, output))
+    grad_filters = filter_results(grads_owned).T
     return (output, grad_out, grad_in, grad_values, grad_filters)
 
 

time: 77.2 us -> 76.4 us (0.990)
  the two profiles are of different devices: /device:TPU:2 before, /device:TPU:32 now
where the time goes in v5:
time: 76.4 us; the launch traced here: 76.1 us
  waiting for transfers between devices  31.4 us (41%)
  starting transfers between devices  27.6 us (36%)
  Pallas kernels  15.4 us (20%)
  between operations  0.79 us (1%)
  local copies, waits for them, and re-layouts  0.77 us (1%)
    all_to_all x1, waiting for transfers between devices, per_device(): lax.all_to_all(sections, 'seq', split_axis=0, concat_axis=0, tiled=True)  14.1 us
    all_to_all x1, waiting for transfers between devices, per_device(): lax.all_to_all(back, 'seq', split_axis=0, concat_axis=0, tiled=True)  13.5 us
    all_to_all x1, starting transfers between devices, per_device(): lax.all_to_all(sections, 'seq', split_axis=0, concat_axis=0, tiled=True)  7.95 us
    ppermute x1, starting transfers between devices, per_device(): filters_here = lax.ppermute(filters_owned, ('seq', 'ch'), swap)  7.73 us
    ppermute x1, starting transfers between devices, per_device(): grads_owned = lax.ppermute(grads, ('seq', 'ch'), swap)  6.64 us
    pallas_call x1, Pallas kernels, convolutions(): pl.pallas_call(functools.partial(convolution_kernel, scale / (LANES * LAN...  6.55 us
    all_to_all x1, starting transfers between devices, per_device(): lax.all_to_all(back, 'seq', split_axis=0, concat_axis=0, tiled=True)  5.28 us
    pallas_call x1, Pallas kernels, filter_spectra(): pl.pallas_call(spectrum_kernel, in_specs=in_vmem(5), out_specs=in_vmem(1)...  4.13 us
  transfers between devices with their start and end apart: 4, of which 4 were waited for; matrix products, arithmetic and copies ran while one was open for 0% of the time, Pallas kernels for 7%

profile of v5, /device:TPU:32, one launch (start us, length us, event | category | flops | bytes accessed | tf_op | source)
XLA Modules:
  0.0 76.1 jit_solution(9183387922233405185)
XLA Ops:
  0.6 2.3 %gate_products.1 = bf16[4,16,2,16,128]{4,3,2,1,0:T(8,128)(2,1)} custom-call(bf16[128,1024]{1,0:T(8,128)(2,1)} %out_gate.3, bf16[128,1024]{1,0:T(8,128)(2,1)} %in_gate.3, bf16[128,1024]{1,0:T(8,128)(2,1)} %values.3, bf16[128,1024]{1,0:T(8,128)(2,1)} %cotan.3), custom_call_target="tpu_custom_call" | custom-call | flops 2000000000 | bytes 1024 | tf_op jit(solution)/shard_map/gate_products/pallas_call | solution.py:43
  3.0 7.7 %collective-permute-start = (bf16[16,8192]{1,0:T(8,128)(2,1)S(1)}, bf16[16,8192]{1,0:T(8,128)(2,1)S(1)}, u32[]{:S(2)}, u32[]{:S(2)}) collective-permute-start(bf16[16,8192]{1,0:T(8,128)(2,1)S(1)} %bitcast.6), channel_id=1, source_target_pairs={{0,0},{1,64},{2,128},{3,192},{4,4},{5,68},{6,132},{7,196},{8,8},{9... | collective-permute-start | bytes 786440 | tf_op jit(solution)/shard_map/ppermute | solution.py:405
  10.7 8.0 %all-to-all-start = ((bf16[64,2,16,128]{3,2,1,0:T(8,128)(2,1)}), bf16[64,2,16,128]{3,2,1,0:T(8,128)(2,1)S(1)}, u32[]{:S(2)}, u32[]{:S(2)}) async-start(bf16[64,2,16,128]{3,2,1,0:T(8,128)(2,1)} %bitcast.5), calls=%async_computation | async-start | bytes 1048576 | tf_op jit(solution)/shard_map/all_to_all | solution.py:408
  18.7 0.0 copy-start.4
  18.7 0.0 copy-start.5
  18.7 0.0 copy-start.6
  18.7 0.0 copy-start.7
  18.7 0.0 copy-start.8
  18.7 0.0 copy-start.9
  18.7 0.0 copy-start.10
  18.8 1.4 %collective-permute-done.filters = bf16[16,8192]{1,0:T(8,128)(2,1)S(1)} collective-permute-done((bf16[16,8192]{1,0:T(8,128)(2,1)S(1)}, bf16[16,8192]{1,0:T(8,128)(2,1)S(1)}, u32[]{:S(2)}, u32[]{:S(2)}) %collective-permute-start) | collective-permute-done | bytes 262176 | tf_op jit(solution)/shard_map/ppermute | solution.py:405
  20.2 0.7 copy-done.12
  20.9 4.1 %filter_spectra.1.spectrum_far = f32[16,128,256]{2,1,0:T(8,128)} custom-call(bf16[16,8192]{1,0:T(8,128)(2,1)} %copy-done.12, bf16[256,128]{1,0:T(8,128)(2,1)} %constant.17.clone.first, bf16[768,256]{1,0:T(8,128)(2,1)} %constant.18.clone.second, f32[128,128]{1,0:T(8,128)} %constant.22.clone.turn_cos, f32[128,128]{1,0:T(8,128)} %constant.23.clone.turn_sin), custom_call_target="tpu_custom_call" | custom-call | flops 12000000000 | bytes 1024 | tf_op jit(solution)/shard_map/filter_spectra/pallas_call | solution.py:291
  25.0 14.1 %all-to-all-done.received = bf16[64,2,16,128]{3,2,1,0:T(8,128)(2,1)S(1)} async-done(((bf16[64,2,16,128]{3,2,1,0:T(8,128)(2,1)}), bf16[64,2,16,128]{3,2,1,0:T(8,128)(2,1)S(1)}, u32[]{:S(2)}, u32[]{:S(2)}) %all-to-all-start) | async-done | bytes 524320 | tf_op jit(solution)/shard_map/all_to_all | solution.py:408
  39.1 0.0 copy-done.7
  39.1 0.0 copy-done.8
  39.1 0.0 copy-done.9
  39.2 6.6 %convolutions.1 = (bf16[64,2,16,128]{3,2,1,0:T(8,128)(2,1)}, bf16[64,16,128]{2,1,0:T(8,128)(2,1)S(1)}) custom-call(bf16[64,2,16,128]{3,2,1,0:T(8,128)(2,1)S(1)} %all-to-all-done.received, f32[16,128,256]{2,1,0:T(8,128)} %filter_spectra.1.spectrum_far, bf16[256,256]{1,0:T(8,128)(2,1)S(1)} %copy-done.7, bf16[768,256]{1,0:T(8,128)(2,1)S(1)} %copy-done.4, ...), custom_call_target="tpu_custom_call" | custom-call | flops 6000000000 | bytes 1024 | tf_op jit(solution)/shard_map/convolutions/pallas_call | solution.py:317
  45.7 5.3 %all-to-all-start.1 = ((bf16[64,2,16,128]{3,2,1,0:T(8,128)(2,1)}), bf16[64,2,16,128]{3,2,1,0:T(8,128)(2,1)S(1)}, u32[]{:S(2)}, u32[]{:S(2)}) async-start(bf16[64,2,16,128]{3,2,1,0:T(8,128)(2,1)} %get-tuple-element.18), calls=%async_computation.1 | async-start | bytes 1048576 | tf_op jit(solution)/shard_map/all_to_all | solution.py:411
  51.0 6.6 %collective-permute-start.1 = (bf16[64,16,128]{2,1,0:T(8,128)(2,1)S(1)}, bf16[64,16,128]{2,1,0:T(8,128)(2,1)S(1)}, u32[]{:S(2)}, u32[]{:S(2)}) collective-permute-start(bf16[64,16,128]{2,1,0:T(8,128)(2,1)S(1)} %get-tuple-element.17), channel_id=1, source_target_pairs={{0,0},{1,64},{2,128},{3,192},{4,4},{5,68},{6,132},{7,196},{8,8},{9... | collective-permute-start | bytes 786440 | tf_op jit(solution)/shard_map/ppermute | solution.py:410
  57.7 13.5 %all-to-all-done.1 = bf16[64,2,16,128]{3,2,1,0:T(8,128)(2,1)S(1)} async-done(((bf16[64,2,16,128]{3,2,1,0:T(8,128)(2,1)}), bf16[64,2,16,128]{3,2,1,0:T(8,128)(2,1)S(1)}, u32[]{:S(2)}, u32[]{:S(2)}) %all-to-all-start.1) | async-done | bytes 524320 | tf_op jit(solution)/shard_map/all_to_all | solution.py:411
  71.2 1.4 %gate_results.1 = (bf16[128,1024]{1,0:T(8,128)(2,1)}, bf16[128,1024]{1,0:T(8,128)(2,1)}, bf16[128,1024]{1,0:T(8,128)(2,1)}, bf16[128,1024]{1,0:T(8,128)(2,1)}) custom-call(bf16[128,1024]{1,0:T(8,128)(2,1)S(1)} %copy-done, bf16[128,1024]{1,0:T(8,128)(2,1)S(1)} %copy-done.1, bf16[128,1024]{1,0:T(8,128)(2,1)S(1)} %copy-done.2, bf16[128,1024]{1,0:T(8,128)(2,1)S(1)} %copy-done.3, ...), custom_call_target="tpu_custom_call" | custom-call | flops 2000000000 | bytes 1024 | tf_op jit(solution)/shard_map/gate_results/pallas_call | solution.py:359
  72.6 2.4 %collective-permute-done.1.received = bf16[64,16,128]{2,1,0:T(8,128)(2,1)S(1)} collective-permute-done((bf16[64,16,128]{2,1,0:T(8,128)(2,1)S(1)}, bf16[64,16,128]{2,1,0:T(8,128)(2,1)S(1)}, u32[]{:S(2)}, u32[]{:S(2)}) %collective-permute-start.1) | collective-permute-done | bytes 262176 | tf_op jit(solution)/shard_map/ppermute | solution.py:410
  75.0 1.0 %filter_results.1 = f32[16,8192]{1,0:T(8,128)} custom-call(bf16[64,16,128]{2,1,0:T(8,128)(2,1)S(1)} %collective-permute-done.1.received), custom_call_target="tpu_custom_call" | custom-call | flops 12000000000 | bytes 1024 | tf_op jit(solution)/shard_map/filter_results/pallas_call | solution.py:382
  (15 shorter events, 0.0 us)
Async XLA Ops:
  0.6 2.3 %copy-start.11 = (bf16[8192,16]{0,1:T(8,128)(2,1)S(1)}, bf16[8192,16]{0,1:T(8,128)(2,1)}, u32[]{:S(2)}) copy-start(bf16[8192,16]{0,1:T(8,128)(2,1)} %param.16) | copy-start | bytes 786436
  3.0 17.2 %collective-permute-start = (bf16[16,8192]{1,0:T(8,128)(2,1)S(1)}, bf16[16,8192]{1,0:T(8,128)(2,1)S(1)}, u32[]{:S(2)}, u32[]{:S(2)}) collective-permute-start(bf16[16,8192]{1,0:T(8,128)(2,1)S(1)} %bitcast.6), channel_id=1, source_target_pairs={{0,0},{1,64},{2,128},{3,192},{4,4},{5,68},{6,132},{7,196},{8,8},{9... | collective-permute-start | bytes 786440 | tf_op jit(solution)/shard_map/ppermute | solution.py:405
  10.7 28.4 %all-to-all-start = ((bf16[64,2,16,128]{3,2,1,0:T(8,128)(2,1)}), bf16[64,2,16,128]{3,2,1,0:T(8,128)(2,1)S(1)}, u32[]{:S(2)}, u32[]{:S(2)}) async-start(bf16[64,2,16,128]{3,2,1,0:T(8,128)(2,1)} %bitcast.5), calls=%async_computation | async-start | bytes 1048576 | tf_op jit(solution)/shard_map/all_to_all | solution.py:408
  18.7 20.4 %copy-start.4 = (bf16[768,256]{1,0:T(8,128)(2,1)S(1)}, bf16[768,256]{1,0:T(8,128)(2,1)}, u32[]{:S(2)}) copy-start(bf16[768,256]{1,0:T(8,128)(2,1)} %constant.18.clone.second) | copy-start | bytes 1179652
  18.7 20.4 %copy-start.5 = (bf16[768,256]{1,0:T(8,128)(2,1)S(1)}, bf16[768,256]{1,0:T(8,128)(2,1)}, u32[]{:S(2)}) copy-start(bf16[768,256]{1,0:T(8,128)(2,1)} %constant.19.clone.second_back) | copy-start | bytes 1179652
  18.7 20.4 %copy-start.6 = (bf16[256,256]{1,0:T(8,128)(2,1)S(1)}, bf16[256,256]{1,0:T(8,128)(2,1)}, u32[]{:S(2)}) copy-start(bf16[256,256]{1,0:T(8,128)(2,1)} %constant.20.clone.first_back) | copy-start | bytes 393220
  18.7 20.4 %copy-start.7 = (bf16[256,256]{1,0:T(8,128)(2,1)S(1)}, bf16[256,256]{1,0:T(8,128)(2,1)}, u32[]{:S(2)}) copy-start(bf16[256,256]{1,0:T(8,128)(2,1)} %constant.16.clone.first) | copy-start | bytes 393220
  18.7 20.4 %copy-start.8 = (f32[128,128]{1,0:T(8,128)S(1)}, f32[128,128]{1,0:T(8,128)}, u32[]{:S(2)}) copy-start(f32[128,128]{1,0:T(8,128)} %constant.23.clone.turn_sin) | copy-start | bytes 196612
  18.7 20.4 %copy-start.9 = (f32[128,128]{1,0:T(8,128)S(1)}, f32[128,128]{1,0:T(8,128)}, u32[]{:S(2)}) copy-start(f32[128,128]{1,0:T(8,128)} %constant.22.clone.turn_cos) | copy-start | bytes 196612
  18.7 20.4 %copy-start.10 = (bf16[128,256]{1,0:T(8,128)(2,1)S(1)}, bf16[128,256]{1,0:T(8,128)(2,1)}, u32[]{:S(2)}) copy-start(bf16[128,256]{1,0:T(8,128)(2,1)} %constant.21.clone.first_back_imag) | copy-start | bytes 196612
  20.2 0.7 copy-start.12
  25.0 46.2 %copy-start = (bf16[128,1024]{1,0:T(8,128)(2,1)S(1)}, bf16[128,1024]{1,0:T(8,128)(2,1)}, u32[]{:S(2)}) copy-start(bf16[128,1024]{1,0:T(8,128)(2,1)} %out_gate.3) | copy-start | bytes 786436
  25.0 46.2 %copy-start.1 = (bf16[128,1024]{1,0:T(8,128)(2,1)S(1)}, bf16[128,1024]{1,0:T(8,128)(2,1)}, u32[]{:S(2)}) copy-start(bf16[128,1024]{1,0:T(8,128)(2,1)} %in_gate.3) | copy-start | bytes 786436
  25.0 46.2 %copy-start.2 = (bf16[128,1024]{1,0:T(8,128)(2,1)S(1)}, bf16[128,1024]{1,0:T(8,128)(2,1)}, u32[]{:S(2)}) copy-start(bf16[128,1024]{1,0:T(8,128)(2,1)} %values.3) | copy-start | bytes 786436
  25.0 46.2 %copy-start.3 = (bf16[128,1024]{1,0:T(8,128)(2,1)S(1)}, bf16[128,1024]{1,0:T(8,128)(2,1)}, u32[]{:S(2)}) copy-start(bf16[128,1024]{1,0:T(8,128)(2,1)} %cotan.3) | copy-start | bytes 786436
  45.7 25.5 %all-to-all-start.1 = ((bf16[64,2,16,128]{3,2,1,0:T(8,128)(2,1)}), bf16[64,2,16,128]{3,2,1,0:T(8,128)(2,1)S(1)}, u32[]{:S(2)}, u32[]{:S(2)}) async-start(bf16[64,2,16,128]{3,2,1,0:T(8,128)(2,1)} %get-tuple-element.18), calls=%async_computation.1 | async-start | bytes 1048576 | tf_op jit(solution)/shard_map/all_to_all | solution.py:411
  51.0 24.0 %collective-permute-start.1 = (bf16[64,16,128]{2,1,0:T(8,128)(2,1)S(1)}, bf16[64,16,128]{2,1,0:T(8,128)(2,1)S(1)}, u32[]{:S(2)}, u32[]{:S(2)}) collective-permute-start(bf16[64,16,128]{2,1,0:T(8,128)(2,1)S(1)} %get-tuple-element.17), channel_id=1, source_target_pairs={{0,0},{1,64},{2,128},{3,192},{4,4},{5,68},{6,132},{7,196},{8,8},{9... | collective-permute-start | bytes 786440 | tf_op jit(solution)/shard_map/ppermute | solution.py:410

commit v6 on v5

--- a/solution.py
+++ b/solution.py
@@ -12,6 +12,7 @@
 LANES = 128
 TOGETHER = 8
 GROUP = 4
+PARTS = 2
 WIDE = jnp.float32
 NARROW = jnp.bfloat16
 
@@ -192,15 +193,10 @@
     turn_sin,
     first_back_imag,
     send_far,
-    grad_filters,
-    filter_spectrum,
-    send,
-    signal,
-    back,
-    grads,
-    loaded,
-    sent,
+    *others,
 ):
+    grad_filters = others[:PARTS]
+    filter_spectrum, send, signal, back, grads, loaded, sent = others[PARTS:]
     blocks, _, owned, _ = received.shape
 
     def load(at):
@@ -255,8 +251,10 @@
 
     lax.fori_loop(0, owned // TOGETHER, pair, 0)
     up = ups[0] * ups[1] * scale
+    members = blocks // PARTS
     for j in range(blocks):
-        grad_filters[j] = (grads[pl.ds(j * owned, owned), :] * up).astype(NARROW)
+        value = grads[pl.ds(j * owned, owned), :] * up
+        grad_filters[j // members][j % members] = value.astype(NARROW)
     up = [one * scale for one in ups]
     pieces = 4
     rows = blocks // pieces
@@ -317,11 +315,11 @@
     return pl.pallas_call(
         functools.partial(convolution_kernel, scale / (LANES * LANES)),
         in_specs=in_vmem(1) + [far] + in_vmem(7),
-        out_specs=[far] + in_vmem(1),
+        out_specs=[far] + in_vmem(PARTS),
         out_shape=[
             jax.ShapeDtypeStruct(received.shape, NARROW),
-            jax.ShapeDtypeStruct((blocks, owned, LANES), NARROW),
-        ],
+        ]
+        + [jax.ShapeDtypeStruct((blocks // PARTS, owned, LANES), NARROW)] * PARTS,
         scratch_shapes=[
             pltpu.VMEM(filter_spectrum.shape, WIDE),
             pltpu.VMEM(received.shape, NARROW),
@@ -369,23 +367,31 @@
     )(out_gate, in_gate, values, cotan, received)
 
 
-def filter_kernel(received, grad_filters):
-    blocks, owned, _ = received.shape
-    flat = received[...].reshape(blocks * owned, LANES)
-    flipped = dot(flat, exchange_matrix()).reshape(blocks, owned, LANES)
-    for j in range(blocks):
-        grad_filters[:, pl.ds(j * LANES, LANES)] = flipped[blocks - 1 - j]
-
-
-def filter_results(received):
-    blocks, owned, _ = received.shape
+def filter_kernel(received, *refs):
+    grad_filters = refs[-1]
+    members, owned, _ = received.shape
+    flat = received[...].reshape(members * owned, LANES)
+    flipped = dot(flat, exchange_matrix()).reshape(members, owned, LANES)
+    for j in range(members):
+        grad_filters[:, pl.ds((members - 1 - j) * LANES, LANES)] = flipped[j]
+
+
+def filter_results(received, part, so_far):
+    members, owned, _ = received.shape
+    width = members * LANES
+    before = [] if so_far is None else [so_far]
     return pl.pallas_call(
         filter_kernel,
-        out_shape=jax.ShapeDtypeStruct((owned, blocks * LANES), WIDE),
+        grid=(1,),
+        in_specs=[pl.BlockSpec(received.shape, lambda i: (0, 0, 0))]
+        + [pl.BlockSpec(memory_space=pl.ANY)] * len(before),
+        out_specs=pl.BlockSpec((owned, width), lambda i: (0, PARTS - 1 - part)),
+        out_shape=jax.ShapeDtypeStruct((owned, PARTS * width), WIDE),
+        input_output_aliases={1: 0} if before else {},
         compiler_params=params(50),
-        cost_estimate=cost(12),
+        cost_estimate=cost(2),
         name="filter_results",
-    )(received)
+    )(received, *before)
 
 
 def per_device(output_gate, input_gate, values_in, filters, cotangent):
@@ -406,15 +412,18 @@
     filter_spectrum = filter_spectra(filters_here, tables)
     sections = send.reshape(seq_count, 2, owned, LANES)
     received = lax.all_to_all(sections, "seq", split_axis=0, concat_axis=0, tiled=True)
-    back, grads = convolutions(received, filter_spectrum, tables, scale)
-    grads_owned = lax.ppermute(grads, ("seq", "ch"), swap)
+    back, *grads = convolutions(received, filter_spectrum, tables, scale)
+    grads_owned = [lax.ppermute(one, ("seq", "ch"), swap) for one in grads]
     returned = lax.all_to_all(back, "seq", split_axis=0, concat_axis=0, tiled=True)
     returned = returned.reshape(chan_count, per_group, 2, owned, LANES)
     output, grad_out, grad_in, grad_values = results(
         output_gate, input_gate, values_in, cotangent, returned
     )
-    grads_owned, output = lax.optimization_barrier((grads_owned, output))
-    grad_filters = filter_results(grads_owned).T
+    grads_owned[0], output = lax.optimization_barrier((grads_owned[0], output))
+    grad_filters = None
+    for part in range(PARTS):
+        grad_filters = filter_results(grads_owned[part], part, grad_filters)
+    grad_filters = grad_filters.T
     return (output, grad_out, grad_in, grad_values, grad_filters)
 
 

time: 76.4 us -> 76.3 us (level)
  waiting for transfers between devices: 31.4 us -> 28.3 us
  starting transfers between devices: 27.6 us -> 29.8 us
  Pallas kernels: 15.4 us -> 16.2 us
    all_to_all x1, waiting for transfers between devices: 13.5 us -> 10.7 us  [per_device(): lax.all_to_all(back, 'seq', split_axis=0, concat_axis=0, tiled=True)]
    ppermute x1 -> x2, starting transfers between devices: 6.64 us -> 8.85 us  [per_device(): grads_owned = [lax.ppermute(one, ('seq', 'ch'), swap) for one in grads]]
    pallas_call x1 -> x2, Pallas kernels: 1.01 us -> 1.75 us  [filter_results(): pl.pallas_call(filter_kernel, grid=(1,), in_specs=[pl.BlockSpec(received....]
    ppermute x1 -> x2, waiting for transfers between devices: 2.41 us -> 2.14 us  [per_device(): grads_owned = [lax.ppermute(one, ('seq', 'ch'), swap) for one in grads]]
  transfers between devices with their start and end apart: 4 -> 5, of which waited for: 4 -> 5; matrix products, arithmetic and copies ran while one was open for 0% -> 0% of each run, Pallas kernels for 7% -> 8%
where the time goes in v6:
time: 76.3 us; the launch traced here: 75.9 us
  starting transfers between devices  29.8 us (39%)
  waiting for transfers between devices  28.3 us (37%)
  Pallas kernels  16.2 us (21%)
  between operations  0.8 us (1%)
  local copies, waits for them, and re-layouts  0.77 us (1%)
    all_to_all x1, waiting for transfers between devices, per_device(): lax.all_to_all(sections, 'seq', split_axis=0, concat_axis=0, tiled=True)  14.1 us
    all_to_all x1, waiting for transfers between devices, per_device(): lax.all_to_all(back, 'seq', split_axis=0, concat_axis=0, tiled=True)  10.7 us
    ppermute x2, starting transfers between devices, per_device(): grads_owned = [lax.ppermute(one, ('seq', 'ch'), swap) for one in grads]  8.85 us
    all_to_all x1, starting transfers between devices, per_device(): lax.all_to_all(sections, 'seq', split_axis=0, concat_axis=0, tiled=True)  7.95 us
    ppermute x1, starting transfers between devices, per_device(): filters_here = lax.ppermute(filters_owned, ('seq', 'ch'), swap)  7.73 us
    pallas_call x1, Pallas kernels, convolutions(): pl.pallas_call(functools.partial(convolution_kernel, scale / (LANES * LAN...  6.55 us
    all_to_all x1, starting transfers between devices, per_device(): lax.all_to_all(back, 'seq', split_axis=0, concat_axis=0, tiled=True)  5.28 us
    pallas_call x1, Pallas kernels, filter_spectra(): pl.pallas_call(spectrum_kernel, in_specs=in_vmem(5), out_specs=in_vmem(1)...  4.12 us
  transfers between devices with their start and end apart: 5, of which 5 were waited for; matrix products, arithmetic and copies ran while one was open for 0% of the time, Pallas kernels for 8%

profile of v6, /device:TPU:32, one launch (start us, length us, event | category | flops | bytes accessed | tf_op | source)
XLA Modules:
  0.0 75.9 jit_solution(5181987917077229797)
XLA Ops:
  0.6 2.3 %gate_products.1 = bf16[4,16,2,16,128]{4,3,2,1,0:T(8,128)(2,1)} custom-call(bf16[128,1024]{1,0:T(8,128)(2,1)} %out_gate.3, bf16[128,1024]{1,0:T(8,128)(2,1)} %in_gate.3, bf16[128,1024]{1,0:T(8,128)(2,1)} %values.3, bf16[128,1024]{1,0:T(8,128)(2,1)} %cotan.3), custom_call_target="tpu_custom_call" | custom-call | flops 2000000000 | bytes 1024 | tf_op jit(solution)/shard_map/gate_products/pallas_call | solution.py:44
  3.0 7.7 %collective-permute-start = (bf16[16,8192]{1,0:T(8,128)(2,1)S(1)}, bf16[16,8192]{1,0:T(8,128)(2,1)S(1)}, u32[]{:S(2)}, u32[]{:S(2)}) collective-permute-start(bf16[16,8192]{1,0:T(8,128)(2,1)S(1)} %bitcast.6), channel_id=1, source_target_pairs={{0,0},{1,64},{2,128},{3,192},{4,4},{5,68},{6,132},{7,196},{8,8},{9... | collective-permute-start | bytes 786440 | tf_op jit(solution)/shard_map/ppermute | solution.py:411
  10.7 8.0 %all-to-all-start = ((bf16[64,2,16,128]{3,2,1,0:T(8,128)(2,1)}), bf16[64,2,16,128]{3,2,1,0:T(8,128)(2,1)S(1)}, u32[]{:S(2)}, u32[]{:S(2)}) async-start(bf16[64,2,16,128]{3,2,1,0:T(8,128)(2,1)} %bitcast.5), calls=%async_computation | async-start | bytes 1048576 | tf_op jit(solution)/shard_map/all_to_all | solution.py:414
  18.7 0.0 copy-start.4
  18.7 0.0 copy-start.5
  18.7 0.0 copy-start.6
  18.7 0.0 copy-start.7
  18.7 0.0 copy-start.8
  18.7 0.0 copy-start.9
  18.7 0.0 copy-start.10
  18.8 1.4 %collective-permute-done.filters = bf16[16,8192]{1,0:T(8,128)(2,1)S(1)} collective-permute-done((bf16[16,8192]{1,0:T(8,128)(2,1)S(1)}, bf16[16,8192]{1,0:T(8,128)(2,1)S(1)}, u32[]{:S(2)}, u32[]{:S(2)}) %collective-permute-start) | collective-permute-done | bytes 262176 | tf_op jit(solution)/shard_map/ppermute | solution.py:411
  20.2 0.7 copy-done.12
  20.9 4.1 %filter_spectra.1.spectrum_far = f32[16,128,256]{2,1,0:T(8,128)} custom-call(bf16[16,8192]{1,0:T(8,128)(2,1)} %copy-done.12, bf16[256,128]{1,0:T(8,128)(2,1)} %constant.17.clone.first, bf16[768,256]{1,0:T(8,128)(2,1)} %constant.18.clone.second, f32[128,128]{1,0:T(8,128)} %constant.22.clone.turn_cos, f32[128,128]{1,0:T(8,128)} %constant.23.clone.turn_sin), custom_call_target="tpu_custom_call" | custom-call | flops 12000000000 | bytes 1024 | tf_op jit(solution)/shard_map/filter_spectra/pallas_call | solution.py:289
  25.0 14.1 %all-to-all-done.received = bf16[64,2,16,128]{3,2,1,0:T(8,128)(2,1)S(1)} async-done(((bf16[64,2,16,128]{3,2,1,0:T(8,128)(2,1)}), bf16[64,2,16,128]{3,2,1,0:T(8,128)(2,1)S(1)}, u32[]{:S(2)}, u32[]{:S(2)}) %all-to-all-start) | async-done | bytes 524320 | tf_op jit(solution)/shard_map/all_to_all | solution.py:414
  39.2 6.6 %convolutions.1 = (bf16[64,2,16,128]{3,2,1,0:T(8,128)(2,1)}, bf16[32,16,128]{2,1,0:T(8,128)(2,1)S(1)}, bf16[32,16,128]{2,1,0:T(8,128)(2,1)S(1)}) custom-call(bf16[64,2,16,128]{3,2,1,0:T(8,128)(2,1)S(1)} %all-to-all-done.received, f32[16,128,256]{2,1,0:T(8,128)} %filter_spectra.1.spectrum_far, bf16[256,256]{1,0:T(8,128)(2,1)S(1)} %copy-done.7, ...), custom_call_target="tpu_custom_call" | custom-call | flops 6000000000 | bytes 1024 | tf_op jit(solution)/shard_map/convolutions/pallas_call | solution.py:315
  45.7 5.3 %all-to-all-start.1 = ((bf16[64,2,16,128]{3,2,1,0:T(8,128)(2,1)}), bf16[64,2,16,128]{3,2,1,0:T(8,128)(2,1)S(1)}, u32[]{:S(2)}, u32[]{:S(2)}) async-start(bf16[64,2,16,128]{3,2,1,0:T(8,128)(2,1)} %get-tuple-element.19), calls=%async_computation.1 | async-start | bytes 1048576 | tf_op jit(solution)/shard_map/all_to_all | solution.py:417
  51.0 6.6 %collective-permute-start.1 = (bf16[32,16,128]{2,1,0:T(8,128)(2,1)S(1)}, bf16[32,16,128]{2,1,0:T(8,128)(2,1)S(1)}, u32[]{:S(2)}, u32[]{:S(2)}) collective-permute-start(bf16[32,16,128]{2,1,0:T(8,128)(2,1)S(1)} %get-tuple-element.18), channel_id=1, source_target_pairs={{0,0},{1,64},{2,128},{3,192},{4,4},{5,68},{6,132},{7,196},{8,8},{9... | collective-permute-start | bytes 393224 | tf_op jit(solution)/shard_map/ppermute | solution.py:416
  57.7 2.2 %collective-permute-start.2 = (bf16[32,16,128]{2,1,0:T(8,128)(2,1)S(1)}, bf16[32,16,128]{2,1,0:T(8,128)(2,1)S(1)}, u32[]{:S(2)}, u32[]{:S(2)}) collective-permute-start(bf16[32,16,128]{2,1,0:T(8,128)(2,1)S(1)} %get-tuple-element.25), channel_id=1, source_target_pairs={{0,0},{1,64},{2,128},{3,192},{4,4},{5,68},{6,132},{7,196},{8,8},{9... | collective-permute-start | bytes 393224 | tf_op jit(solution)/shard_map/ppermute | solution.py:416
  59.9 10.7 %all-to-all-done.1 = bf16[64,2,16,128]{3,2,1,0:T(8,128)(2,1)S(1)} async-done(((bf16[64,2,16,128]{3,2,1,0:T(8,128)(2,1)}), bf16[64,2,16,128]{3,2,1,0:T(8,128)(2,1)S(1)}, u32[]{:S(2)}, u32[]{:S(2)}) %all-to-all-start.1) | async-done | bytes 524320 | tf_op jit(solution)/shard_map/all_to_all | solution.py:417
  70.6 1.4 %gate_results.1 = (bf16[128,1024]{1,0:T(8,128)(2,1)}, bf16[128,1024]{1,0:T(8,128)(2,1)}, bf16[128,1024]{1,0:T(8,128)(2,1)}, bf16[128,1024]{1,0:T(8,128)(2,1)}) custom-call(bf16[128,1024]{1,0:T(8,128)(2,1)S(1)} %copy-done, bf16[128,1024]{1,0:T(8,128)(2,1)S(1)} %copy-done.1, bf16[128,1024]{1,0:T(8,128)(2,1)S(1)} %copy-done.2, bf16[128,1024]{1,0:T(8,128)(2,1)S(1)} %copy-done.3, ...), custom_call_target="tpu_custom_call" | custom-call | flops 2000000000 | bytes 1024 | tf_op jit(solution)/shard_map/gate_results/pallas_call | solution.py:357
  72.0 1.5 %collective-permute-done.1.received = bf16[32,16,128]{2,1,0:T(8,128)(2,1)S(1)} collective-permute-done((bf16[32,16,128]{2,1,0:T(8,128)(2,1)S(1)}, bf16[32,16,128]{2,1,0:T(8,128)(2,1)S(1)}, u32[]{:S(2)}, u32[]{:S(2)}) %collective-permute-start.1) | collective-permute-done | bytes 131104 | tf_op jit(solution)/shard_map/ppermute | solution.py:416
  73.5 0.9 %filter_results.2.refs_0_ = f32[16,8192]{1,0:T(8,128)} custom-call(bf16[32,16,128]{2,1,0:T(8,128)(2,1)S(1)} %collective-permute-done.1.received), custom_call_target="tpu_custom_call" | custom-call | flops 2000000000 | bytes 1024 | tf_op jit(solution)/shard_map/filter_results/pallas_call | solution.py:383
  74.4 0.6 collective-permute-done.2.received
  75.0 0.9 %filter_results.3 = f32[16,8192]{1,0:T(8,128)} custom-call(bf16[32,16,128]{2,1,0:T(8,128)(2,1)S(1)} %collective-permute-done.2.received, f32[16,8192]{1,0:T(8,128)} %filter_results.2.refs_0_), custom_call_target="tpu_custom_call", output_to_operand_aliasing={{}: (1, {})} | custom-call | flops 2000000000 | bytes 1024 | tf_op jit(solution)/shard_map/filter_results/pallas_call | solution.py:383
  (18 shorter events, 0.0 us)
Async XLA Ops:
  0.6 2.3 %copy-start.11 = (bf16[8192,16]{0,1:T(8,128)(2,1)S(1)}, bf16[8192,16]{0,1:T(8,128)(2,1)}, u32[]{:S(2)}) copy-start(bf16[8192,16]{0,1:T(8,128)(2,1)} %param.16) | copy-start | bytes 786436
  3.0 17.2 %collective-permute-start = (bf16[16,8192]{1,0:T(8,128)(2,1)S(1)}, bf16[16,8192]{1,0:T(8,128)(2,1)S(1)}, u32[]{:S(2)}, u32[]{:S(2)}) collective-permute-start(bf16[16,8192]{1,0:T(8,128)(2,1)S(1)} %bitcast.6), channel_id=1, source_target_pairs={{0,0},{1,64},{2,128},{3,192},{4,4},{5,68},{6,132},{7,196},{8,8},{9... | collective-permute-start | bytes 786440 | tf_op jit(solution)/shard_map/ppermute | solution.py:411
  10.7 28.4 %all-to-all-start = ((bf16[64,2,16,128]{3,2,1,0:T(8,128)(2,1)}), bf16[64,2,16,128]{3,2,1,0:T(8,128)(2,1)S(1)}, u32[]{:S(2)}, u32[]{:S(2)}) async-start(bf16[64,2,16,128]{3,2,1,0:T(8,128)(2,1)} %bitcast.5), calls=%async_computation | async-start | bytes 1048576 | tf_op jit(solution)/shard_map/all_to_all | solution.py:414
  18.7 20.4 %copy-start.4 = (bf16[768,256]{1,0:T(8,128)(2,1)S(1)}, bf16[768,256]{1,0:T(8,128)(2,1)}, u32[]{:S(2)}) copy-start(bf16[768,256]{1,0:T(8,128)(2,1)} %constant.18.clone.second) | copy-start | bytes 1179652
  18.7 20.4 %copy-start.5 = (bf16[768,256]{1,0:T(8,128)(2,1)S(1)}, bf16[768,256]{1,0:T(8,128)(2,1)}, u32[]{:S(2)}) copy-start(bf16[768,256]{1,0:T(8,128)(2,1)} %constant.19.clone.second_back) | copy-start | bytes 1179652
  18.7 20.4 %copy-start.6 = (bf16[256,256]{1,0:T(8,128)(2,1)S(1)}, bf16[256,256]{1,0:T(8,128)(2,1)}, u32[]{:S(2)}) copy-start(bf16[256,256]{1,0:T(8,128)(2,1)} %constant.20.clone.first_back) | copy-start | bytes 393220
  18.7 20.4 %copy-start.7 = (bf16[256,256]{1,0:T(8,128)(2,1)S(1)}, bf16[256,256]{1,0:T(8,128)(2,1)}, u32[]{:S(2)}) copy-start(bf16[256,256]{1,0:T(8,128)(2,1)} %constant.16.clone.first) | copy-start | bytes 393220
  18.7 20.4 %copy-start.8 = (f32[128,128]{1,0:T(8,128)S(1)}, f32[128,128]{1,0:T(8,128)}, u32[]{:S(2)}) copy-start(f32[128,128]{1,0:T(8,128)} %constant.23.clone.turn_sin) | copy-start | bytes 196612
  18.7 20.4 %copy-start.9 = (f32[128,128]{1,0:T(8,128)S(1)}, f32[128,128]{1,0:T(8,128)}, u32[]{:S(2)}) copy-start(f32[128,128]{1,0:T(8,128)} %constant.22.clone.turn_cos) | copy-start | bytes 196612
  18.7 20.4 %copy-start.10 = (bf16[128,256]{1,0:T(8,128)(2,1)S(1)}, bf16[128,256]{1,0:T(8,128)(2,1)}, u32[]{:S(2)}) copy-start(bf16[128,256]{1,0:T(8,128)(2,1)} %constant.21.clone.first_back_imag) | copy-start | bytes 196612
  20.2 0.7 copy-start.12
  25.0 45.6 %copy-start = (bf16[128,1024]{1,0:T(8,128)(2,1)S(1)}, bf16[128,1024]{1,0:T(8,128)(2,1)}, u32[]{:S(2)}) copy-start(bf16[128,1024]{1,0:T(8,128)(2,1)} %out_gate.3) | copy-start | bytes 786436
  25.0 45.6 %copy-start.1 = (bf16[128,1024]{1,0:T(8,128)(2,1)S(1)}, bf16[128,1024]{1,0:T(8,128)(2,1)}, u32[]{:S(2)}) copy-start(bf16[128,1024]{1,0:T(8,128)(2,1)} %in_gate.3) | copy-start | bytes 786436
  25.0 45.6 %copy-start.2 = (bf16[128,1024]{1,0:T(8,128)(2,1)S(1)}, bf16[128,1024]{1,0:T(8,128)(2,1)}, u32[]{:S(2)}) copy-start(bf16[128,1024]{1,0:T(8,128)(2,1)} %values.3) | copy-start | bytes 786436
  25.0 45.6 %copy-start.3 = (bf16[128,1024]{1,0:T(8,128)(2,1)S(1)}, bf16[128,1024]{1,0:T(8,128)(2,1)}, u32[]{:S(2)}) copy-start(bf16[128,1024]{1,0:T(8,128)(2,1)} %cotan.3) | copy-start | bytes 786436
  45.7 24.9 %all-to-all-start.1 = ((bf16[64,2,16,128]{3,2,1,0:T(8,128)(2,1)}), bf16[64,2,16,128]{3,2,1,0:T(8,128)(2,1)S(1)}, u32[]{:S(2)}, u32[]{:S(2)}) async-start(bf16[64,2,16,128]{3,2,1,0:T(8,128)(2,1)} %get-tuple-element.19), calls=%async_computation.1 | async-start | bytes 1048576 | tf_op jit(solution)/shard_map/all_to_all | solution.py:417
  51.0 22.5 %collective-permute-start.1 = (bf16[32,16,128]{2,1,0:T(8,128)(2,1)S(1)}, bf16[32,16,128]{2,1,0:T(8,128)(2,1)S(1)}, u32[]{:S(2)}, u32[]{:S(2)}) collective-permute-start(bf16[32,16,128]{2,1,0:T(8,128)(2,1)S(1)} %get-tuple-element.18), channel_id=1, source_target_pairs={{0,0},{1,64},{2,128},{3,192},{4,4},{5,68},{6,132},{7,196},{8,8},{9... | collective-permute-start | bytes 393224 | tf_op jit(solution)/shard_map/ppermute | solution.py:416
  57.7 17.4 %collective-permute-start.2 = (bf16[32,16,128]{2,1,0:T(8,128)(2,1)S(1)}, bf16[32,16,128]{2,1,0:T(8,128)(2,1)S(1)}, u32[]{:S(2)}, u32[]{:S(2)}) collective-permute-start(bf16[32,16,128]{2,1,0:T(8,128)(2,1)S(1)} %get-tuple-element.25), channel_id=1, source_target_pairs={{0,0},{1,64},{2,128},{3,192},{4,4},{5,68},{6,132},{7,196},{8,8},{9... | collective-permute-start | bytes 393224 | tf_op jit(solution)/shard_map/ppermute | solution.py:416
